TPU v7x, 32 devices: a whole 2x2x4 slice. The times are simulated.
32 devices in a mesh: dp: 4 (over y, core), tensor: 8 (over z, x).
Axes of the slice: x: 2, y: 2, z: 4, core: 2. Of those that a mesh axis runs over, the one named last changes fastest.
Arguments:
- tokens: bfloat16 [1024, 8192], P('dp', 'tensor'), may hold values from -6 to 6
- pattern: int32 [256, 8], P('tensor'), may hold values from 0 to 63, as said below
- first_blocks: bfloat16 [256, 8, 128, 128], P('tensor'), may hold values from -0.1875 to 0.1875
- second_blocks: bfloat16 [256, 8, 128, 128], P('tensor'), may hold values from -0.1875 to 0.1875
- out_grad: bfloat16 [1024, 8192], P('dp', 'tensor'), may hold values from -0.75 to 0.75
Outputs:
- layer_out: bfloat16 [1024, 8192], P('dp', 'tensor')
- input_grad: bfloat16 [1024, 8192], P('dp', 'tensor')
- first_grad: bfloat16 [256, 8, 128, 128], P('tensor')
- second_grad: bfloat16 [256, 8, 128, 128], P('tensor')
Inputs may be any that keep to these rules, and one draw needn't show every extreme that they name: `pattern`: each hidden block row r lists 8 distinct feature blocks: r mod 64, the blocks that differ from it in bit 0, in bit 3 and in the highest bit, and 4 further ones drawn at random. Every feature block is listed by some row.
All inputs are finite; a program needn't handle non-finite values.
Results may differ from a plain program's by a relative error of at most 0.015.
Values may be sent and summed in bfloat16 or wider, within the bound.
No kernel may reach another device: no remote copies, remote signals or barrier semaphores. Data moves between devices by JAX's collectives and lax.ppermute only.
A program may use at most 192 MiB of HBM per device.

v0:
```python
import jax
import jax.numpy as jnp
from jax import lax
from jax.sharding import PartitionSpec as P

gelu_scale = 0.7978845608028654
gelu_cube = 0.044715


def gelu_pair(value):
    inner = gelu_scale * (value + gelu_cube * value * value * value)
    tangent = jnp.tanh(inner)
    result = 0.5 * value * (1.0 + tangent)
    slope = 0.5 * (1.0 + tangent) + 0.5 * value * (1.0 - tangent * tangent) * gelu_scale * (
        1.0 + 3.0 * gelu_cube * value * value
    )
    return (result, slope)


def place_blocks(terms, pattern, count):
    targets = jnp.arange(count, dtype=jnp.int32)
    select = (pattern[:, :, None] == targets[None, None, :]).astype(jnp.float32)
    return jnp.einsum("trkc,rkf->ftc", terms, select, precision=lax.Precision.HIGHEST)


def shards(tokens, pattern, first_blocks, second_blocks, out_grad):
    tok_rows = tokens.shape[0]
    block_size = first_blocks.shape[-1]
    group_size = lax.axis_size("tensor")
    feat_blocks = tokens.shape[1] * group_size // block_size
    own_blocks = feat_blocks // group_size
    full_tokens = lax.all_gather(tokens, "tensor", axis=1, tiled=True).reshape(
        tok_rows, feat_blocks, block_size
    )
    picked = full_tokens[:, pattern, :]
    pre = jnp.einsum("trki,rkio->tro", picked, first_blocks, preferred_element_type=jnp.float32)
    value, slope = gelu_pair(pre)
    active = value.astype(jnp.bfloat16)
    contrib = jnp.einsum(
        "tro,rkoc->trkc", active, second_blocks, preferred_element_type=jnp.float32
    )
    out_terms = place_blocks(contrib, pattern, feat_blocks)
    out_rows = lax.psum_scatter(
        out_terms.astype(jnp.bfloat16), "tensor", scatter_dimension=0, tiled=True
    ).astype(jnp.float32)
    layer_out = (
        jnp.transpose(out_rows, (1, 0, 2))
        .reshape(tok_rows, own_blocks * block_size)
        .astype(jnp.bfloat16)
    )
    full_grad = lax.all_gather(out_grad, "tensor", axis=1, tiled=True).reshape(
        tok_rows, feat_blocks, block_size
    )
    grad_picked = full_grad[:, pattern, :]
    second_term = jnp.einsum(
        "tro,trkc->rkoc", active, grad_picked, preferred_element_type=jnp.float32
    )
    act_grad = jnp.einsum(
        "trkc,rkoc->tro", grad_picked, second_blocks, preferred_element_type=jnp.float32
    )
    pre_grad = (act_grad * slope).astype(jnp.bfloat16)
    first_term = jnp.einsum("trki,tro->rkio", picked, pre_grad, preferred_element_type=jnp.float32)
    back_term = jnp.einsum(
        "tro,rkio->trki", pre_grad, first_blocks, preferred_element_type=jnp.float32
    )
    back_terms = place_blocks(back_term, pattern, feat_blocks)
    back_rows = lax.psum_scatter(
        back_terms.astype(jnp.bfloat16), "tensor", scatter_dimension=0, tiled=True
    ).astype(jnp.float32)
    input_grad = (
        jnp.transpose(back_rows, (1, 0, 2))
        .reshape(tok_rows, own_blocks * block_size)
        .astype(jnp.bfloat16)
    )
    first_total, second_total = (
        lax.psum(first_term.astype(jnp.bfloat16), "dp").astype(jnp.float32),
        lax.psum(second_term.astype(jnp.bfloat16), "dp").astype(jnp.float32),
    )
    first_grad = first_total.astype(jnp.bfloat16)
    second_grad = second_total.astype(jnp.bfloat16)
    return (layer_out, input_grad, first_grad, second_grad)


def solution(mesh):
    placed = (
        P("dp", "tensor"),
        P("tensor", None),
        P("tensor", None, None, None),
        P("tensor", None, None, None),
        P("dp", "tensor"),
    )
    return jax.shard_map(
        shards,
        mesh=mesh,
        in_specs=placed,
        out_specs=(
            P("dp", "tensor"),
            P("dp", "tensor"),
            P("tensor", None, None, None),
            P("tensor", None, None, None),
        ),
        check_vma=False,
    )
```

profile of v0, /device:TPU:0, one launch (start us, length us, event | category | flops | bytes accessed | tf_op | source)
XLA Modules:
  0.0 775.0 jit_solution(8942118986014088308)
XLA Ops:
  9.3 2.0 copy.38
  12.3 74.5 %all-gather.3.cloned.1.call-done = bf16[256,8192]{0,1:T(8,128)(2,1)} async-done(((bf16[256,1024]{0,1:T(8,128)(2,1)}), bf16[256,8192]{0,1:T(8,128)(2,1)}) %all-gather.3.cloned.1.call-update) | async-done | bytes 4194320 | tf_op jit(solution)/shard_map/all_gather | solution.py:32
  86.8 6.4 copy.34
  93.2 68.0 %all-gather.5.cloned.1.call-done = bf16[256,8192]{0,1:T(8,128)(2,1)} async-done(((bf16[256,1024]{0,1:T(8,128)(2,1)}), bf16[256,8192]{0,1:T(8,128)(2,1)}) %all-gather.5.cloned.1.call-update) | async-done | bytes 4194320 | tf_op jit(solution)/shard_map/all_gather | solution.py:51
  161.2 6.4 copy.39
  167.6 12.0 %gather_fusion.1 = bf16[256,256,128]{2,1,0:T(8,128)(2,1)} fusion(bf16[256,64,128]{2,0,1:T(8,128)(2,1)} %copy.39, s32[1024]{0:T(1024)S(1)} %pad_clamp_fusion), kind=kCustom, calls=%fused_computation.1 | custom fusion | bytes 33555456 | tf_op jit(solution)/shard_map/gather | solution.py:54
  179.5 12.0 %gather_fusion = bf16[256,256,128]{2,1,0:T(8,128)(2,1)} fusion(bf16[256,64,128]{2,0,1:T(8,128)(2,1)} %copy.34, s32[1024]{0:T(1024)S(1)} %pad_clamp_fusion), kind=kCustom, calls=%fused_computation | custom fusion | bytes 33555456 | tf_op jit(solution)/shard_map/gather | solution.py:35
  191.5 22.5 %copy.35 = bf16[32,8,256,128]{2,3,1,0:T(8,128)(2,1)} copy(bf16[32,8,256,128]{3,2,1,0:T(8,128)(2,1)} %bitcast.112) | data formatting | bytes 33554432 | tf_op jit(solution)/shard_map/gather | solution.py:35
  214.1 22.5 %copy.40 = bf16[32,8,256,128]{2,3,1,0:T(8,128)(2,1)} copy(bf16[32,8,256,128]{3,2,1,0:T(8,128)(2,1)} %bitcast.110) | data formatting | bytes 33554432 | tf_op jit(solution)/shard_map/gather | solution.py:54
  236.6 14.7 %fusion.35 = f32[32,256,128,1]{2,1,3,0:T(8,128)} fusion(bf16[256,32,8,128]{3,0,2,1:T(8,128)(2,1)} %bitcast.113, bf16[32,8,128,128]{3,2,1,0:T(8,128)(2,1)} %param.7), kind=kOutput, calls=%fused_computation.43 | convolution fusion | flops 2147483648 | bytes 29360128 | tf_op jit(solution)/shard_map/trki,rkio->tro/dot_general | solution.py:36
  251.2 11.5 %convert_bitcast_fusion = bf16[32,8,128,128]{2,3,1,0:T(8,128)(2,1)} fusion(bf16[32,8,256,128]{2,3,1,0:T(8,128)(2,1)} %copy.40, f32[32,256,128,1]{2,1,3,0:T(8,128)} %fusion.35), kind=kOutput, calls=%fused_computation.14 | convolution fusion | flops 2161115136 | bytes 29360128 | tf_op jit(solution)/shard_map/tro,trkc->rkoc/dot_general | solution.py:55
  262.7 12.3 %fusion.19 = bf16[256,32,128]{2,0,1:T(8,128)(2,1)S(1)} fusion(f32[32,256,128,1]{2,1,3,0:T(8,128)} %fusion.35, bf16[256,32,8,128]{3,0,2,1:T(8,128)(2,1)} %bitcast.111, bf16[32,8,128,128]{3,2,1,0:T(8,128)(2,1)} %param.8), kind=kOutput, calls=%fused_computation.24 | convolution fusion | flops 2167406592 | bytes 31457280 | tf_op jit(solution)/shard_map/trkc,rkoc->tro/dot_general | solution.py:58
  275.1 10.2 %fusion.8 = bf16[32,8,128,128]{3,2,1,0:T(8,128)(2,1)} fusion(bf16[32,8,256,128]{2,3,1,0:T(8,128)(2,1)} %copy.35, bf16[256,32,128]{2,0,1:T(8,128)(2,1)S(1)} %fusion.19), kind=kOutput, calls=%fused_computation.15 | convolution fusion | flops 2151677952 | bytes 27262976 | tf_op jit(solution)/shard_map/trki,tro->rkio/dot_general | solution.py:62
  285.3 21.5 %convolution_bitcast_fusion.1 = f32[256,32,8,128]{3,0,2,1:T(8,128)} fusion(bf16[32,8,128,128]{3,2,1,0:T(8,128)(2,1)} %param.8, f32[32,256,128,1]{2,1,3,0:T(8,128)} %fusion.35), kind=kOutput, calls=%fused_computation.11 | convolution fusion | flops 2156920832 | bytes 46137344 | tf_op jit(solution)/shard_map/tro,rkoc->trkc/dot_general | solution.py:39
  306.8 60.0 %fusion.20 = bf16[256,8,8,128]{3,2,1,0:T(8,128)(2,1)} fusion(f32[256,32,8,128]{3,0,2,1:T(8,128)} %convolution_bitcast_fusion.1, s32[32,8]{0,1:T(8,128)S(1)} %copy-done), kind=kOutput, calls=%fused_computation.25 | convolution fusion | flops 6444564480 | bytes 37749760 | tf_op jit(solution)/shard_map/trkc,rkf->ftc/dot_general | solution.py:23
  366.9 5.0 copy.77
  371.9 17.3 %convolution_bitcast_fusion = f32[256,32,8,128]{3,0,2,1:T(8,128)} fusion(bf16[32,8,128,128]{3,2,1,0:T(8,128)(2,1)} %param.7, bf16[256,32,128]{2,0,1:T(8,128)(2,1)S(1)} %fusion.19), kind=kOutput, calls=%fused_computation.10 | convolution fusion | flops 2147483648 | bytes 44040192 | tf_op jit(solution)/shard_map/tro,rkio->trki/dot_general | solution.py:63
  389.3 48.6 %fusion.21 = bf16[256,8,8,128]{3,2,1,0:T(8,128)(2,1)} fusion(f32[256,32,8,128]{3,0,2,1:T(8,128)} %convolution_bitcast_fusion, s32[32,8]{0,1:T(8,128)S(1)} %copy-done), kind=kOutput, calls=%fused_computation.26 | convolution fusion | flops 6444564480 | bytes 37749760 | tf_op jit(solution)/shard_map/trkc,rkf->ftc/dot_general | solution.py:23
  437.9 5.0 copy.76
  442.9 129.6 %all-reduce.3.cloned.1.call-done = (bf16[32,8,128,128]{3,2,1,0:T(8,128)(2,1)}, bf16[32,8,128,128]{2,3,1,0:T(8,128)(2,1)}) async-done(((bf16[32,8,128,128]{3,2,1,0:T(8,128)(2,1)}, bf16[32,8,128,128]{2,3,1,0:T(8,128)(2,1)}), (bf16[32,8,128,128]{3,2,1,0:T(8,128)(2,1)}, bf16[32,8,128,128]{2,3,1,0:T(8,128)(2,1)})) %all-reduce.3.cloned.1.call-update) | async-done | bytes 16777232 | tf_op jit(solution)/shard_map/psum | solution.py:76
  572.5 11.9 %copy.43 = bf16[32,8,128,128]{3,2,1,0:T(8,128)(2,1)} copy(bf16[32,8,128,128]{2,3,1,0:T(8,128)(2,1)} %get-tuple-element.21) | data formatting | bytes 16777216
  584.4 79.5 %reduce-scatter.7.cloned.1.call-done = bf16[8,32768]{1,0:T(8,128)(2,1)} async-done(((bf16[64,32768]{1,0:T(8,128)(2,1)}), bf16[8,32768]{1,0:T(8,128)(2,1)}) %reduce-scatter.7.cloned.1.call-update) | async-done | bytes 524304
  665.9 89.7 %reduce-scatter.9.cloned.1.call-done = bf16[8,32768]{1,0:T(8,128)(2,1)} async-done(((bf16[64,32768]{1,0:T(8,128)(2,1)}), bf16[8,32768]{1,0:T(8,128)(2,1)}) %reduce-scatter.9.cloned.1.call-update) | async-done | bytes 524304
  757.5 10.5 %copy.82 = bf16[32,8,128,128]{3,2,1,0:T(8,128)(2,1)} copy(bf16[32,8,128,128]{3,2,1,0:T(8,128)(2,1)} %get-tuple-element.24) | data formatting | bytes 16777216
  (19 shorter events, 7.1 us)
Async XLA Ops:
  7.2 79.7 %all-gather.3.cloned.1.call-start = ((), (), s32[]{:S(2)}) async-start(), calls=%async_computation.2 | async-start | bytes 4718592 | tf_op jit(solution)/shard_map/all_gather | solution.py:32
  9.3 151.9 %all-gather.5.cloned.1.call-start = ((), (), s32[]{:S(2)}) async-start(), calls=%async_computation.3 | async-start | bytes 4718592 | tf_op jit(solution)/shard_map/all_gather | solution.py:51
  11.4 561.1 %all-reduce.3.cloned.1.call-start = ((), (), s32[]{:S(2)}) async-start(), calls=%async_computation.6 | async-start | bytes 33554432 | tf_op jit(solution)/shard_map/psum | solution.py:76
  285.2 21.6 %copy-start = (s32[32,8]{0,1:T(8,128)S(1)}, s32[32,8]{0,1:T(8,128)}, u32[]{:S(2)}) copy-start(s32[32,8]{0,1:T(8,128)} %param.6) | copy-start | bytes 3076
  285.2 378.7 %reduce-scatter.7.cloned.1.call-start = ((), (), s32[]{:S(2)}) async-start(), calls=%async_computation.4 | async-start | bytes 4718592
  371.9 383.7 %reduce-scatter.9.cloned.1.call-start = ((), (), s32[]{:S(2)}) async-start(), calls=%async_computation.5 | async-start | bytes 4718592
Sparse Core Ops, SparseCore 0:
  10.7 76.0 all-gather.2
  89.5 71.6 all-gather.4
  285.3 287.1 all-reduce.2
  576.0 87.8 reduce-scatter.6
  667.8 87.6 reduce-scatter.8
where the time goes:
time: 786 us; the launch traced here: 775 us
  waiting for transfers between devices  441 us (56%)
  matrix products  196 us (25%)
  local copies, waits for them, and re-layouts  122 us (16%)
  between operations  14.3 us (2%)
    unnamed x7, waiting for transfers between devices  169 us
    psum x1, waiting for transfers between devices, shards(): lax.psum(first_term.astype(jnp.bfloat16), 'dp').astype(jnp.float32)  130 us
    dot_general x2, matrix products, place_blocks(): jnp.einsum('trkc,rkf->ftc', terms, select, precision=lax.Precision.HIGHEST)  109 us
    all_gather x1, waiting for transfers between devices, shards(): lax.all_gather(tokens, 'tensor', axis=1, tiled=True)  74.5 us
    all_gather x1, waiting for transfers between devices, shards(): lax.all_gather(out_grad, 'tensor', axis=1, tiled=True)  68 us
    unnamed x10, local copies, waits for them, and re-layouts  40.4 us
    gather x2, local copies, waits for them, and re-layouts, shards(): picked = full_tokens[:, pattern, :]  34.5 us
    gather x2, local copies, waits for them, and re-layouts, shards(): grad_picked = full_grad[:, pattern, :]  34.5 us
  transfers between devices with their start and end apart: 5, of which 5 were waited for; matrix products, arithmetic and copies ran while one was open for 23% of the time, Pallas kernels for 0%

commit v1 on v0

v1 whole, which is shorter than its diff:
```python
import functools

import jax
import jax.numpy as jnp
from jax import lax
from jax.experimental import pallas as pl
from jax.experimental.pallas import tpu as pltpu
from jax.sharding import PartitionSpec as P

gelu_scale = 0.7978845608028654
gelu_cube = 0.044715
BF = jnp.bfloat16
F32 = jnp.float32
ANY = pl.BlockSpec(memory_space=pl.ANY)
VMEM_BYTES = 56 * 1024 * 1024


def gelu_pair(value):
    inner = gelu_scale * (value + gelu_cube * value * value * value)
    tangent = jnp.tanh(inner)
    result = 0.5 * value * (1.0 + tangent)
    slope = 0.5 * (1.0 + tangent) + 0.5 * value * (1.0 - tangent * tangent) * gelu_scale * (
        1.0 + 3.0 * gelu_cube * value * value
    )
    return (result, slope)


def line_pairs(line, step, first, last):
    return [
        (a * 2 + s, (a + step) * 2 + s)
        for a in range(first, last + 1)
        for s in range(2)
        if 0 <= a + step < line
    ]


def swap_pairs(first, last):
    return [(a * 2 + s, a * 2 + 1 - s) for a in range(first, last + 1) for s in range(2)]


def gather_parts(own, line):
    held = {0: own}
    for k in range(1, line):
        held[-k] = lax.ppermute(held[1 - k], "tensor", line_pairs(line, 1, k - 1, line - 2))
        held[k] = lax.ppermute(held[k - 1], "tensor", line_pairs(line, -1, 1, line - k))
    parts = []
    for d in range(1 - line, line):
        across = lax.ppermute(held[d], "tensor", swap_pairs(max(0, -d), min(line - 1, line - 1 - d)))
        parts += [held[d], across]
    return parts


def scatter_sum(send, keep, line):
    got = [lax.ppermute(send[k], "tensor", swap_pairs(0, line - 1)) for k in range(line)]
    both = [keep[k].astype(F32) + got[k].astype(F32) for k in range(line)]
    up = down = None
    for k in range(line - 1, 0, -1):
        load_up, load_down = both[k], both[line - k]
        if up is not None:
            load_up, load_down = load_up + up.astype(F32), load_down + down.astype(F32)
        up = lax.ppermute(load_up.astype(BF), "tensor", line_pairs(line, 1, 0, line - 1 - k))
        down = lax.ppermute(load_down.astype(BF), "tensor", line_pairs(line, -1, k, line - 1))
    total = both[0]
    if up is not None:
        total = total + up.astype(F32) + down.astype(F32)
    return total.astype(BF)


def core_swap(value):
    count = lax.axis_size("dp")
    return lax.ppermute(value, "dp", [(i, i ^ 1) for i in range(count)])


def ring_sum(value):
    count = lax.axis_size("dp")
    total = value.astype(F32)
    for s in range(2, count, 2):
        total = total + lax.ppermute(value, "dp", [(i, (i + s) % count) for i in range(count)]).astype(F32)
    return total.astype(BF)


def load_parts(meta, refs, full, sem, line):
    at, side = meta[0], meta[1]
    for n, ref in enumerate(refs):
        place = at + n // 2 - (line - 1)

        @pl.when((place >= 0) & (place < line))
        def _(ref=ref, place=place, other=n % 2):
            slot = place * 2 + (side if other == 0 else 1 - side)
            pltpu.make_async_copy(ref, full.at[slot], sem).start()


def wait_parts(full, sem):
    pltpu.make_async_copy(full, full, sem).wait()


def block_at(pat, row, j, blocks, own_blocks, size):
    block = pat[row * blocks + j]
    return block // own_blocks, pl.ds(pl.multiple_of((block % own_blocks) * size, size), size)


def pick(full, pat, row, blocks, size):
    own_blocks = full.shape[-1] // size
    pieces = []
    for j in range(blocks):
        shard, lanes = block_at(pat, row, j, blocks, own_blocks, size)
        pieces.append(full[shard, :, lanes])
    return jnp.concatenate(pieces, axis=1)


def forward_kernel(line, n_parts, meta, pat, *refs):
    parts, (w_ref, act_ref, slope_ref, full, sem) = refs[:n_parts], refs[n_parts:]
    row = pl.program_id(0)

    @pl.when(row == 0)
    def _():
        load_parts(meta, parts, full, sem, line)
        wait_parts(full, sem)

    _, blocks, size, _ = w_ref.shape
    picked = pick(full, pat, row, blocks, size)
    pre = jnp.dot(picked, w_ref[0].reshape(blocks * size, size), preferred_element_type=F32)
    value, slope = gelu_pair(pre)
    act_ref[0] = value.astype(BF)
    slope_ref[0] = slope


def forward(meta, pat, parts, weights, line):
    rows, blocks, size, _ = weights.shape
    tok, width = parts[0].shape
    shards = 2 * line
    spec = pl.BlockSpec((1, tok, size), lambda r, *_: (r, 0, 0))
    return pl.pallas_call(
        functools.partial(forward_kernel, line, len(parts)),
        grid_spec=pltpu.PrefetchScalarGridSpec(
            num_scalar_prefetch=2,
            grid=(rows,),
            in_specs=[ANY] * len(parts)
            + [pl.BlockSpec((1, blocks, size, size), lambda r, *_: (r, 0, 0, 0))],
            out_specs=[spec, spec],
            scratch_shapes=[pltpu.VMEM((shards, tok, width), BF), pltpu.SemaphoreType.DMA],
        ),
        out_shape=[
            jax.ShapeDtypeStruct((rows, tok, size), BF),
            jax.ShapeDtypeStruct((rows, tok, size), F32),
        ],
        compiler_params=pltpu.CompilerParams(vmem_limit_bytes=VMEM_BYTES),
        cost_estimate=pl.CostEstimate(
            flops=2 * rows * blocks * tok * size * size,
            bytes_accessed=2 * weights.size + 2 * shards * tok * width + 6 * rows * tok * size,
            transcendentals=rows * tok * size,
        ),
        name="forward_rows",
    )(meta, pat, *parts, weights)


def spread_kernel(flip, line, meta, pat, in_ref, w_ref, send_ref, keep_ref, acc):
    row = pl.program_id(0)
    _, blocks, size, _ = w_ref.shape
    own_blocks = acc.shape[-1] // size

    @pl.when(row == 0)
    def _():
        acc[...] = jnp.zeros_like(acc)

    value = in_ref[0]
    if flip:
        weight = w_ref[0].reshape(blocks * size, size)
        terms = lax.dot_general(value, weight, (((1,), (1,)), ((), ())), preferred_element_type=F32)
    else:
        weight = jnp.concatenate([w_ref[0, j] for j in range(blocks)], axis=1)
        terms = jnp.dot(value, weight, preferred_element_type=F32)
    for j in range(blocks):
        shard, lanes = block_at(pat, row, j, blocks, own_blocks, size)
        acc[shard, :, lanes] += terms[:, j * size : (j + 1) * size]

    @pl.when(row == pl.num_programs(0) - 1)
    def _():
        at, side = meta[0], meta[1]
        for k in range(line):
            place = lax.rem(at + k, line)
            send_ref[k] = acc[place * 2 + 1 - side].astype(BF)
            keep_ref[k] = acc[place * 2 + side].astype(BF)


def spread(flip, meta, pat, values, weights, line, width):
    rows, blocks, size, _ = weights.shape
    tok = values.shape[1]
    whole = pl.BlockSpec((line, tok, width), lambda r, *_: (0, 0, 0))
    return pl.pallas_call(
        functools.partial(spread_kernel, flip, line),
        grid_spec=pltpu.PrefetchScalarGridSpec(
            num_scalar_prefetch=2,
            grid=(rows,),
            in_specs=[
                pl.BlockSpec((1, tok, size), lambda r, *_: (r, 0, 0)),
                pl.BlockSpec((1, blocks, size, size), lambda r, *_: (r, 0, 0, 0)),
            ],
            out_specs=[whole, whole],
            scratch_shapes=[pltpu.VMEM((2 * line, tok, width), F32)],
        ),
        out_shape=[jax.ShapeDtypeStruct((line, tok, width), BF)] * 2,
        compiler_params=pltpu.CompilerParams(vmem_limit_bytes=VMEM_BYTES),
        cost_estimate=pl.CostEstimate(
            flops=2 * rows * blocks * tok * size * size,
            bytes_accessed=2 * weights.size + 2 * values.size + 4 * line * tok * width,
            transcendentals=0,
        ),
        name="spread_back" if flip else "spread_out",
    )(meta, pat, values, weights)


def chunk_row(start, half, meta, i, rows):
    core = meta[2] if half == 0 else 1 - meta[2]
    return core * (rows // 2) + start + i


def chunk_kernel(line, n_parts, start, half, rows, add, chained, meta, pat, *refs):
    g_parts, x_parts, refs = refs[:n_parts], refs[n_parts : 2 * n_parts], refs[2 * n_parts :]
    act_ref, slope_ref, w_ref = refs[:3]
    refs = refs[3:]
    if add:
        more_second, more_first = refs[:2]
        refs = refs[2:]
    if chained:
        refs = refs[1:]
    second_ref, first_ref, pg_ref, g_full, x_full, g_sem, x_sem = refs
    step = pl.program_id(0)
    row = chunk_row(start, half, meta, step, rows)
    _, blocks, size, _ = w_ref.shape

    @pl.when(step == 0)
    def _():
        load_parts(meta, g_parts, g_full, g_sem, line)
        load_parts(meta, x_parts, x_full, x_sem, line)
        wait_parts(g_full, g_sem)

    act = act_ref[0]
    grads = pick(g_full, pat, row, blocks, size)
    second = lax.dot_general(act, grads, (((0,), (0,)), ((), ())), preferred_element_type=F32)
    for j in range(blocks):
        term = second[:, j * size : (j + 1) * size]
        if add:
            term = term.astype(BF).astype(F32) + more_second[0, j].astype(F32)
        second_ref[0, j] = term.astype(BF)
    weight = jnp.concatenate([w_ref[0, j] for j in range(blocks)], axis=1)
    act_grad = lax.dot_general(grads, weight, (((1,), (1,)), ((), ())), preferred_element_type=F32)
    pre_grad = (act_grad * slope_ref[0]).astype(BF)
    pg_ref[0] = pre_grad

    @pl.when(step == 0)
    def _():
        wait_parts(x_full, x_sem)

    picked = pick(x_full, pat, row, blocks, size)
    first = lax.dot_general(picked, pre_grad, (((0,), (0,)), ((), ())), preferred_element_type=F32)
    for j in range(blocks):
        term = first[j * size : (j + 1) * size]
        if add:
            term = term.astype(BF).astype(F32) + more_first[0, j].astype(F32)
        first_ref[0, j] = term.astype(BF)


def chunk(meta, pat, g_parts, x_parts, act, slope, weights, more, pg, start, count, half, line):
    rows, blocks, size, _ = weights.shape
    tok, width = g_parts[0].shape
    n = len(g_parts)

    def at_row(r, meta, pat):
        return (chunk_row(start, half, meta, r, rows), 0, 0)

    row_spec = pl.BlockSpec((1, tok, size), at_row)
    block_spec = pl.BlockSpec((1, blocks, size, size), lambda r, *_: (r, 0, 0, 0))
    w_spec = pl.BlockSpec((1, blocks, size, size), lambda r, m, p: at_row(r, m, p) + (0,))
    args = [*g_parts, *x_parts, act, slope, weights]
    specs = [ANY] * (2 * n) + [row_spec, row_spec, w_spec]
    if more is not None:
        args += list(more)
        specs += [block_spec, block_spec]
    aliases = {}
    if pg is not None:
        aliases = {2 + len(args): 2}
        args.append(pg)
        specs.append(ANY)
    grad = jax.ShapeDtypeStruct((count, blocks, size, size), BF)
    return pl.pallas_call(
        functools.partial(chunk_kernel, line, n, start, half, rows, more is not None, pg is not None),
        grid_spec=pltpu.PrefetchScalarGridSpec(
            num_scalar_prefetch=2,
            grid=(count,),
            in_specs=specs,
            out_specs=[block_spec, block_spec, row_spec],
            scratch_shapes=[
                pltpu.VMEM((2 * line, tok, width), BF),
                pltpu.VMEM((2 * line, tok, width), BF),
                pltpu.SemaphoreType.DMA,
                pltpu.SemaphoreType.DMA,
            ],
        ),
        out_shape=[grad, grad, jax.ShapeDtypeStruct((rows, tok, size), BF)],
        input_output_aliases=aliases,
        compiler_params=pltpu.CompilerParams(vmem_limit_bytes=VMEM_BYTES),
        cost_estimate=pl.CostEstimate(
            flops=6 * count * blocks * tok * size * size,
            bytes_accessed=8 * line * tok * width + 6 * count * blocks * size * size,
            transcendentals=0,
        ),
        name="grad_rows",
    )(meta, pat, *args)


def shards(tokens, pattern, first_blocks, second_blocks, out_grad):
    rows, blocks, size, _ = first_blocks.shape
    width = tokens.shape[1]
    line = lax.axis_size("tensor") // 2
    place = lax.axis_index("tensor")
    core = lax.axis_index("dp") % 2
    meta = jnp.stack([place // 2, place % 2, core]).astype(jnp.int32)
    pat = pattern.reshape(-1)

    x_parts = gather_parts(tokens, line)
    g_parts = gather_parts(out_grad, line)
    act, slope = forward(meta, pat, x_parts, first_blocks, line)
    out_send, out_keep = spread(False, meta, pat, act, second_blocks, line, width)

    half_rows = rows // 2
    count = max(1, half_rows // 4)
    starts = list(range(0, half_rows, count))
    run = functools.partial(chunk, meta, pat, g_parts, x_parts, act, slope, second_blocks)
    pg = None
    sent, kept = {}, {}
    for n in range(len(starts) + 1):
        if n < len(starts):
            second, first, pg = run(None, pg, starts[n], count, 1, line)
            sent[n] = (core_swap(second), core_swap(first))
        if n > 0:
            second, first, pg = run(sent[n - 1], pg, starts[n - 1], count, 0, line)
            kept[n - 1] = (second, first)
    back_send, back_keep = spread(True, meta, pat, pg, first_blocks, line, width)

    layer_out = scatter_sum(out_send, out_keep, line)
    input_grad = scatter_sum(back_send, back_keep, line)

    totals = [jnp.zeros(first_blocks.shape, BF), jnp.zeros(first_blocks.shape, BF)]
    for n, start in enumerate(starts):
        for which in range(2):
            own = ring_sum(kept[n][which])
            other = core_swap(own)
            total = totals[which]
            total = lax.dynamic_update_slice(total, own, (core * half_rows + start, 0, 0, 0))
            total = lax.dynamic_update_slice(total, other, ((1 - core) * half_rows + start, 0, 0, 0))
            totals[which] = total
    return (layer_out, input_grad, totals[1], totals[0])


def solution(mesh):
    placed = (
        P("dp", "tensor"),
        P("tensor", None),
        P("tensor", None, None, None),
        P("tensor", None, None, None),
        P("dp", "tensor"),
    )
    return jax.shard_map(
        shards,
        mesh=mesh,
        in_specs=placed,
        out_specs=(
            P("dp", "tensor"),
            P("dp", "tensor"),
            P("tensor", None, None, None),
            P("tensor", None, None, None),
        ),
        check_vma=False,
    )
```

time: 786 us -> 479 us (0.61)
  waiting for transfers between devices: 441 us -> 136 us
  matrix products: 196 us -> 0 us
  Pallas kernels: 0 us -> 165 us
  starting transfers between devices: 0.21 us -> 89.3 us
  local copies, waits for them, and re-layouts: 122 us -> 39.2 us
  other arithmetic: 0.7 us -> 44.8 us
  between operations: 14.3 us -> 1.37 us
    dot_general x8 -> x0, matrix products: 196 us -> none  [the longest x2 109 us: place_blocks(): jnp.einsum('trkc,rkf->ftc', terms, select, precision=lax.Precision.HIGHEST)]
    unnamed x7 -> x0, waiting for transfers between devices: 169 us -> none
    pallas_call x0 -> x11, Pallas kernels: none -> 165 us  [the longest x8 83 us: chunk(): pl.pallas_call(functools.partial(chunk_kernel, line, n, start, half, rows...]
    all_gather x2 -> x0, waiting for transfers between devices: 143 us -> none  [the longest x1 74.5 us: shards(): lax.all_gather(tokens, 'tensor', axis=1, tiled=True)]
    ppermute x0 -> x70, waiting for transfers between devices: none -> 136 us  [the longest x8 61.3 us: ring_sum(): lax.ppermute(value, 'dp', [(i, (i + s) % count) for i in range(count)])]
    psum x1 -> x0, waiting for transfers between devices: 130 us -> none  [shards(): lax.psum(first_term.astype(jnp.bfloat16), 'dp').astype(jnp.float32)]
    ppermute x0 -> x70, starting transfers between devices: none -> 89.3 us  [the longest x14 25.5 us: gather_parts(): lax.ppermute(held[d], 'tensor', swap_pairs(max(0, -d), min(line - 1, line...]
    gather x4 -> x0, local copies, waits for them, and re-layouts: 69 us -> none  [the longest x2 34.5 us: shards(): picked = full_tokens[:, pattern, :]]
  transfers between devices with their start and end apart: 5 -> 70, of which waited for: 5 -> 23; matrix products, arithmetic and copies ran while one was open for 23% -> 16% of each run, Pallas kernels for 0% -> 28%
where the time goes in v1:
time: 479 us; the launch traced here: 475 us
  Pallas kernels  165 us (34%)
  waiting for transfers between devices  136 us (28%)
  starting transfers between devices  89.3 us (19%)
  other arithmetic  44.8 us (9%)
  local copies, waits for them, and re-layouts  39.2 us (8%)
    pallas_call x8, Pallas kernels, chunk(): pl.pallas_call(functools.partial(chunk_kernel, line, n, start, half, rows...  83 us
    ppermute x8, waiting for transfers between devices, ring_sum(): lax.ppermute(value, 'dp', [(i, (i + s) % count) for i in range(count)])  61.3 us
    pallas_call x2, Pallas kernels, spread(): pl.pallas_call(functools.partial(spread_kernel, flip, line), grid_spec=pl...  55.2 us
    pallas_call x1, Pallas kernels, forward(): pl.pallas_call(functools.partial(forward_kernel, line, len(parts)), grid_...  26.6 us
    ppermute x6, waiting for transfers between devices, gather_parts(): lax.ppermute(held[k - 1], 'tensor', line_pairs(line, -1, 1, line - k))  26.3 us
    ppermute x14, starting transfers between devices, gather_parts(): lax.ppermute(held[d], 'tensor', swap_pairs(max(0, -d), min(line - 1, line...  25.5 us
    ppermute x8, waiting for transfers between devices, scatter_sum(): lax.ppermute(send[k], 'tensor', swap_pairs(0, line - 1))  21.3 us
    dynamic_update_slice x8, other arithmetic, shards(): lax.dynamic_update_slice(total, own, (core * half_rows + start, 0, 0, 0))  20.1 us
  transfers between devices with their start and end apart: 70, of which 23 were waited for; matrix products, arithmetic and copies ran while one was open for 16% of the time, Pallas kernels for 28%

profile of v1, /device:TPU:0, one launch (start us, length us, event | category | flops | bytes accessed | tf_op | source)
XLA Modules:
  0.0 475.1 jit_solution(8837898916471458728)
XLA Ops:
  37.2 5.8 %collective-permute-done.8.refs_9_.refs_23_ = bf16[256,1024]{1,0:T(8,128)(2,1)S(1)} collective-permute-done((bf16[256,1024]{1,0:T(8,128)(2,1)S(1)}, bf16[256,1024]{1,0:T(8,128)(2,1)S(1)}, u32[]{:S(2)}, u32[]{:S(2)}) %collective-permute-start.8) | collective-permute-done | bytes 524320 | tf_op jit(solution)/shard_map/ppermute | solution.py:48
  52.0 7.3 %collective-permute-done.32.refs_10_ = bf16[256,1024]{1,0:T(8,128)(2,1)} collective-permute-done((bf16[256,1024]{1,0:T(8,128)(2,1)}, bf16[256,1024]{1,0:T(8,128)(2,1)}, u32[]{:S(2)}, u32[]{:S(2)}) %collective-permute-start.32) | collective-permute-done | bytes 524320 | tf_op jit(solution)/shard_map/ppermute | solution.py:45
  62.9 6.4 %collective-permute-done.11.refs_12_.refs_26_ = bf16[256,1024]{1,0:T(8,128)(2,1)S(1)} collective-permute-done((bf16[256,1024]{1,0:T(8,128)(2,1)S(1)}, bf16[256,1024]{1,0:T(8,128)(2,1)S(1)}, u32[]{:S(2)}, u32[]{:S(2)}) %collective-permute-start.11) | collective-permute-done | bytes 524320 | tf_op jit(solution)/shard_map/ppermute | solution.py:45
  76.7 6.0 %collective-permute-done.34.refs_12_ = bf16[256,1024]{1,0:T(8,128)(2,1)} collective-permute-done((bf16[256,1024]{1,0:T(8,128)(2,1)}, bf16[256,1024]{1,0:T(8,128)(2,1)}, u32[]{:S(2)}, u32[]{:S(2)}) %collective-permute-start.34) | collective-permute-done | bytes 524320 | tf_op jit(solution)/shard_map/ppermute | solution.py:45
  92.3 26.6 %forward_rows.1 = (bf16[32,256,128]{2,1,0:T(8,128)(2,1)}, f32[32,256,128]{2,1,0:T(8,128)}) custom-call(s32[3]{0:T(128)} %pad_add_fusion.meta, s32[256]{0:T(256)} %reshape.27.pat, bf16[256,1024]{1,0:T(8,128)(2,1)} %copy-done.7, bf16[256,1024]{1,0:T(8,128)(2,1)} %copy-done.11, bf16[256,1024]{1,0:T(8,128)(2,1)} %copy-done.3, bf16[256,1024]{1,0:T(8,128)(2,1)} %copy-done.8, ...), custom_call_target="tpu_custom_call" | custom-call | flops 2147483648 | bytes 18874368 | tf_op jit(solution)/shard_map/forward_rows/pallas_call | solution.py:133
  119.0 10.1 %grad_rows.8 = (bf16[4,8,128,128]{3,2,1,0:T(8,128)(2,1)}, bf16[4,8,128,128]{3,2,1,0:T(8,128)(2,1)}, bf16[32,256,128]{2,1,0:T(8,128)(2,1)}) custom-call(s32[3]{0:T(128)} %pad_add_fusion.meta, s32[256]{0:T(256)} %reshape.27.pat, bf16[256,1024]{1,0:T(8,128)(2,1)} %collective-permute-done.25.refs_0_, bf16[256,1024]{1,0:T(8,128)(2,1)} %collective-permute-done.26.refs_1_, ...), custom_call_target="tpu_custom_call" | custom-call | flops 805306368 | bytes 11534336 | tf_op jit(solution)/shard_map/grad_rows/pallas_call | solution.py:286
  129.7 10.1 %grad_rows.9 = (bf16[4,8,128,128]{3,2,1,0:T(8,128)(2,1)}, bf16[4,8,128,128]{3,2,1,0:T(8,128)(2,1)}, bf16[32,256,128]{2,1,0:T(8,128)(2,1)}) custom-call(s32[3]{0:T(128)} %pad_add_fusion.meta, s32[256]{0:T(256)} %reshape.27.pat, bf16[256,1024]{1,0:T(8,128)(2,1)} %collective-permute-done.25.refs_0_, ...), custom_call_target="tpu_custom_call", output_to_operand_aliasing={{2}: (33, {})} | custom-call | flops 805306368 | bytes 11534336 | tf_op jit(solution)/shard_map/grad_rows/pallas_call | solution.py:286
  140.4 27.4 %spread_out.1 = (bf16[4,256,1024]{2,1,0:T(8,128)(2,1)}, bf16[4,256,1024]{2,1,0:T(8,128)(2,1)}) custom-call(s32[3]{0:T(128)} %pad_add_fusion.meta, s32[256]{0:T(256)} %reshape.27.pat, bf16[32,256,128]{2,1,0:T(8,128)(2,1)} %get-tuple-element.34.in_ref.refs_28_, bf16[32,8,128,128]{3,2,1,0:T(8,128)(2,1)} %refs_30_.15), custom_call_target="tpu_custom_call" | custom-call | flops 2147483648 | bytes 14680064 | tf_op jit(solution)/shard_map/spread_out/pallas_call | solution.py:190
  169.2 10.5 %grad_rows.10 = (bf16[4,8,128,128]{3,2,1,0:T(8,128)(2,1)}, bf16[4,8,128,128]{3,2,1,0:T(8,128)(2,1)}, bf16[32,256,128]{2,1,0:T(8,128)(2,1)}) custom-call(s32[3]{0:T(128)} %pad_add_fusion.meta, s32[256]{0:T(256)} %reshape.27.pat, bf16[256,1024]{1,0:T(8,128)(2,1)} %collective-permute-done.25.refs_0_, ...), custom_call_target="tpu_custom_call", output_to_operand_aliasing={{2}: (35, {})} | custom-call | flops 805306368 | bytes 11534336 | tf_op jit(solution)/shard_map/grad_rows/pallas_call | solution.py:286
  179.6 10.2 %grad_rows.11 = (bf16[4,8,128,128]{3,2,1,0:T(8,128)(2,1)}, bf16[4,8,128,128]{3,2,1,0:T(8,128)(2,1)}, bf16[32,256,128]{2,1,0:T(8,128)(2,1)}) custom-call(s32[3]{0:T(128)} %pad_add_fusion.meta, s32[256]{0:T(256)} %reshape.27.pat, bf16[256,1024]{1,0:T(8,128)(2,1)} %collective-permute-done.25.refs_0_, ...), custom_call_target="tpu_custom_call", output_to_operand_aliasing={{2}: (33, {})} | custom-call | flops 805306368 | bytes 11534336 | tf_op jit(solution)/shard_map/grad_rows/pallas_call | solution.py:286
  191.1 10.4 %grad_rows.12 = (bf16[4,8,128,128]{3,2,1,0:T(8,128)(2,1)}, bf16[4,8,128,128]{3,2,1,0:T(8,128)(2,1)}, bf16[32,256,128]{2,1,0:T(8,128)(2,1)}) custom-call(s32[3]{0:T(128)} %pad_add_fusion.meta, s32[256]{0:T(256)} %reshape.27.pat, bf16[256,1024]{1,0:T(8,128)(2,1)} %collective-permute-done.25.refs_0_, ...), custom_call_target="tpu_custom_call", output_to_operand_aliasing={{2}: (35, {})} | custom-call | flops 805306368 | bytes 11534336 | tf_op jit(solution)/shard_map/grad_rows/pallas_call | solution.py:286
  201.6 10.6 %grad_rows.13 = (bf16[4,8,128,128]{3,2,1,0:T(8,128)(2,1)}, bf16[4,8,128,128]{3,2,1,0:T(8,128)(2,1)}, bf16[32,256,128]{2,1,0:T(8,128)(2,1)}) custom-call(s32[3]{0:T(128)} %pad_add_fusion.meta, s32[256]{0:T(256)} %reshape.27.pat, bf16[256,1024]{1,0:T(8,128)(2,1)} %collective-permute-done.25.refs_0_, ...), custom_call_target="tpu_custom_call", output_to_operand_aliasing={{2}: (33, {})} | custom-call | flops 805306368 | bytes 11534336 | tf_op jit(solution)/shard_map/grad_rows/pallas_call | solution.py:286
  215.0 13.6 %collective-permute-done.16 = bf16[256,1024]{1,0:T(8,128)(2,1)S(1)} collective-permute-done((bf16[256,1024]{1,0:T(8,128)(2,1)}, bf16[256,1024]{1,0:T(8,128)(2,1)S(1)}, u32[]{:S(2)}, u32[]{:S(2)}) %collective-permute-start.16) | collective-permute-done | bytes 524320 | tf_op jit(solution)/shard_map/ppermute | solution.py:54
  233.2 10.6 %grad_rows.14 = (bf16[4,8,128,128]{3,2,1,0:T(8,128)(2,1)}, bf16[4,8,128,128]{3,2,1,0:T(8,128)(2,1)}, bf16[32,256,128]{2,1,0:T(8,128)(2,1)}) custom-call(s32[3]{0:T(128)} %pad_add_fusion.meta, s32[256]{0:T(256)} %reshape.27.pat, bf16[256,1024]{1,0:T(8,128)(2,1)} %collective-permute-done.25.refs_0_, ...), custom_call_target="tpu_custom_call", output_to_operand_aliasing={{2}: (35, {})} | custom-call | flops 805306368 | bytes 11534336 | tf_op jit(solution)/shard_map/grad_rows/pallas_call | solution.py:286
  247.2 10.5 %grad_rows.15 = (bf16[4,8,128,128]{3,2,1,0:T(8,128)(2,1)}, bf16[4,8,128,128]{3,2,1,0:T(8,128)(2,1)}, bf16[32,256,128]{2,1,0:T(8,128)(2,1)}) custom-call(s32[3]{0:T(128)} %pad_add_fusion.meta, s32[256]{0:T(256)} %reshape.27.pat, bf16[256,1024]{1,0:T(8,128)(2,1)} %collective-permute-done.25.refs_0_, ...), custom_call_target="tpu_custom_call", output_to_operand_aliasing={{2}: (35, {})} | custom-call | flops 805306368 | bytes 11534336 | tf_op jit(solution)/shard_map/grad_rows/pallas_call | solution.py:286
  257.7 27.7 %spread_back.1 = (bf16[4,256,1024]{2,1,0:T(8,128)(2,1)}, bf16[4,256,1024]{2,1,0:T(8,128)(2,1)}) custom-call(s32[3]{0:T(128)} %pad_add_fusion.meta, s32[256]{0:T(256)} %reshape.27.pat, bf16[32,256,128]{2,1,0:T(8,128)(2,1)} %get-tuple-element.53.in_ref, bf16[32,8,128,128]{3,2,1,0:T(8,128)(2,1)} %w_ref.3), custom_call_target="tpu_custom_call" | custom-call | flops 2147483648 | bytes 14680064 | tf_op jit(solution)/shard_map/spread_back/pallas_call | solution.py:190
  293.7 5.5 %broadcast.6.clone = bf16[32,8,128,128]{3,2,1,0:T(8,128)(2,1)} broadcast(bf16[]{:T(256)} %constant.50.clone.1), dimensions={} | broadcast | bytes 8388610 | tf_op jit(solution)/shard_map/broadcast.1
  308.8 5.5 %broadcast.6.clone.1 = bf16[32,8,128,128]{3,2,1,0:T(8,128)(2,1)} broadcast(bf16[]{:T(256)} %constant.50.clone.1), dimensions={} | broadcast | bytes 8388610 | tf_op jit(solution)/shard_map/broadcast.1
  338.9 15.0 %collective-permute-done.64 = bf16[4,8,128,128]{3,2,1,0:T(8,128)(2,1)S(1)} collective-permute-done((bf16[4,8,128,128]{3,2,1,0:T(8,128)(2,1)}, bf16[4,8,128,128]{3,2,1,0:T(8,128)(2,1)S(1)}, u32[]{:S(2)}, u32[]{:S(2)}) %collective-permute-start.64) | collective-permute-done | bytes 1048608 | tf_op jit(solution)/shard_map/ppermute | solution.py:78
  383.7 15.1 %collective-permute-done.66 = bf16[4,8,128,128]{3,2,1,0:T(8,128)(2,1)S(1)} collective-permute-done((bf16[4,8,128,128]{3,2,1,0:T(8,128)(2,1)}, bf16[4,8,128,128]{3,2,1,0:T(8,128)(2,1)S(1)}, u32[]{:S(2)}, u32[]{:S(2)}) %collective-permute-start.66) | collective-permute-done | bytes 1048608 | tf_op jit(solution)/shard_map/ppermute | solution.py:78
  410.4 11.0 %collective-permute-done.60 = bf16[4,8,128,128]{3,2,1,0:T(8,128)(2,1)} collective-permute-done((bf16[4,8,128,128]{3,2,1,0:T(8,128)(2,1)}, bf16[4,8,128,128]{3,2,1,0:T(8,128)(2,1)}, u32[]{:S(2)}, u32[]{:S(2)}) %collective-permute-start.60) | collective-permute-done | bytes 1048608 | tf_op jit(solution)/shard_map/ppermute | solution.py:78
  429.4 13.9 %collective-permute-done.68 = bf16[4,8,128,128]{3,2,1,0:T(8,128)(2,1)S(1)} collective-permute-done((bf16[4,8,128,128]{3,2,1,0:T(8,128)(2,1)}, bf16[4,8,128,128]{3,2,1,0:T(8,128)(2,1)S(1)}, u32[]{:S(2)}, u32[]{:S(2)}) %collective-permute-start.68) | collective-permute-done | bytes 1048608 | tf_op jit(solution)/shard_map/ppermute | solution.py:78
  456.1 5.8 %collective-permute-done.44 = bf16[256,1024]{1,0:T(8,128)(2,1)S(1)} collective-permute-done((bf16[256,1024]{1,0:T(8,128)(2,1)}, bf16[256,1024]{1,0:T(8,128)(2,1)S(1)}, u32[]{:S(2)}, u32[]{:S(2)}) %collective-permute-start.44) | collective-permute-done | bytes 524320 | tf_op jit(solution)/shard_map/ppermute | solution.py:54
  461.9 6.1 %collective-permute-done.53 = bf16[256,1024]{1,0:T(8,128)(2,1)} collective-permute-done((bf16[256,1024]{1,0:T(8,128)(2,1)}, bf16[256,1024]{1,0:T(8,128)(2,1)}, u32[]{:S(2)}, u32[]{:S(2)}) %collective-permute-start.53) | collective-permute-done | bytes 524320 | tf_op jit(solution)/shard_map/ppermute | solution.py:62
  (226 shorter events, 192.1 us)
Async XLA Ops:
  71.8 47.2 %collective-permute-start.31 = (bf16[256,1024]{1,0:T(8,128)(2,1)}, bf16[256,1024]{1,0:T(8,128)(2,1)}, u32[]{:S(2)}, u32[]{:S(2)}) collective-permute-start(bf16[256,1024]{1,0:T(8,128)(2,1)} %collective-permute-done.30.refs_8_), channel_id=1, source_target_pairs={{0,1},{1,0},{2,3},{3,2},{4,5},{5,4},{8,9},{9,8},{10,11},{11,10},{1... | collective-permute-start | bytes 1572872 | tf_op jit(solution)/shard_map/ppermute | solution.py:48
  75.2 43.7 %collective-permute-start.27 = (bf16[256,1024]{1,0:T(8,128)(2,1)}, bf16[256,1024]{1,0:T(8,128)(2,1)}, u32[]{:S(2)}, u32[]{:S(2)}) collective-permute-start(bf16[256,1024]{1,0:T(8,128)(2,1)} %collective-permute-done.24.refs_2_), channel_id=1, source_target_pairs={{4,5},{5,4},{6,7},{7,6},{12,13},{13,12},{14,15},{15,14},{20,21},{2... | collective-permute-start | bytes 1572872 | tf_op jit(solution)/shard_map/ppermute | solution.py:48
  82.7 36.3 %collective-permute-start.33 = (bf16[256,1024]{1,0:T(8,128)(2,1)}, bf16[256,1024]{1,0:T(8,128)(2,1)}, u32[]{:S(2)}, u32[]{:S(2)}) collective-permute-start(bf16[256,1024]{1,0:T(8,128)(2,1)} %collective-permute-done.32.refs_10_), channel_id=1, source_target_pairs={{0,1},{1,0},{2,3},{3,2},{8,9},{9,8},{10,11},{11,10},{16,17},{17,16... | collective-permute-start | bytes 1572872 | tf_op jit(solution)/shard_map/ppermute | solution.py:48
  129.2 38.7 %collective-permute-start.38 = (bf16[4,8,128,128]{3,2,1,0:T(8,128)(2,1)}, bf16[4,8,128,128]{3,2,1,0:T(8,128)(2,1)S(1)}, u32[]{:S(2)}, u32[]{:S(2)}) collective-permute-start(bf16[4,8,128,128]{3,2,1,0:T(8,128)(2,1)} %get-tuple-element.41), channel_id=1, source_target_pairs={{0,8},{8,0},{16,24},{24,16},{1,9},{9,1},{17,25},{25,17},{2,10},{10... | collective-permute-start | bytes 3145736 | tf_op jit(solution)/shard_map/ppermute | solution.py:71
  129.2 38.6 %collective-permute-start.39 = (bf16[4,8,128,128]{3,2,1,0:T(8,128)(2,1)}, bf16[4,8,128,128]{3,2,1,0:T(8,128)(2,1)S(1)}, u32[]{:S(2)}, u32[]{:S(2)}) collective-permute-start(bf16[4,8,128,128]{3,2,1,0:T(8,128)(2,1)} %get-tuple-element.42), channel_id=1, source_target_pairs={{0,8},{8,0},{16,24},{24,16},{1,9},{9,1},{17,25},{25,17},{2,10},{10... | collective-permute-start | bytes 3145736 | tf_op jit(solution)/shard_map/ppermute | solution.py:71
  139.8 50.0 %collective-permute-start.36 = (bf16[4,8,128,128]{3,2,1,0:T(8,128)(2,1)}, bf16[4,8,128,128]{3,2,1,0:T(8,128)(2,1)S(1)}, u32[]{:S(2)}, u32[]{:S(2)}) collective-permute-start(bf16[4,8,128,128]{3,2,1,0:T(8,128)(2,1)} %get-tuple-element.39), channel_id=1, source_target_pairs={{0,8},{8,0},{16,24},{24,16},{1,9},{9,1},{17,25},{25,17},{2,10},{10... | collective-permute-start | bytes 3145736 | tf_op jit(solution)/shard_map/ppermute | solution.py:71
  140.0 49.9 %collective-permute-start.37 = (bf16[4,8,128,128]{3,2,1,0:T(8,128)(2,1)}, bf16[4,8,128,128]{3,2,1,0:T(8,128)(2,1)S(1)}, u32[]{:S(2)}, u32[]{:S(2)}) collective-permute-start(bf16[4,8,128,128]{3,2,1,0:T(8,128)(2,1)} %get-tuple-element.40), channel_id=1, source_target_pairs={{0,8},{8,0},{16,24},{24,16},{1,9},{9,1},{17,25},{25,17},{2,10},{10... | collective-permute-start | bytes 3145736 | tf_op jit(solution)/shard_map/ppermute | solution.py:71
  212.4 34.4 %collective-permute-start.41 = (bf16[4,8,128,128]{3,2,1,0:T(8,128)(2,1)}, bf16[4,8,128,128]{3,2,1,0:T(8,128)(2,1)}, u32[]{:S(2)}, u32[]{:S(2)}) collective-permute-start(bf16[4,8,128,128]{3,2,1,0:T(8,128)(2,1)} %get-tuple-element.48), channel_id=1, source_target_pairs={{0,8},{8,0},{16,24},{24,16},{1,9},{9,1},{17,25},{25,17},{2,10},{10... | collective-permute-start | bytes 3145736 | tf_op jit(solution)/shard_map/ppermute | solution.py:71
  228.6 64.6 %collective-permute-start.54 = (bf16[4,8,128,128]{3,2,1,0:T(8,128)(2,1)}, bf16[4,8,128,128]{3,2,1,0:T(8,128)(2,1)S(1)}, u32[]{:S(2)}, u32[]{:S(2)}) collective-permute-start(bf16[4,8,128,128]{3,2,1,0:T(8,128)(2,1)} %get-tuple-element.56), channel_id=1, source_target_pairs={{0,16},{8,24},{16,0},{24,8},{1,17},{9,25},{17,1},{25,9},{2,18},{10... | collective-permute-start | bytes 3145736 | tf_op jit(solution)/shard_map/ppermute | solution.py:78
  231.2 57.1 %collective-permute-start.15 = (bf16[256,1024]{1,0:T(8,128)(2,1)S(1)}, bf16[256,1024]{1,0:T(8,128)(2,1)S(1)}, u32[]{:S(2)}, u32[]{:S(2)}) collective-permute-start(bf16[256,1024]{1,0:T(8,128)(2,1)S(1)} %get-tuple-element.90), channel_id=1, source_target_pairs={{0,1},{1,0},{2,3},{3,2},{4,5},{5,4},{6,7},{7,6},{8,9},{9,8},{10,11... | collective-permute-start | bytes 1572872 | tf_op jit(solution)/shard_map/ppermute | solution.py:54
  231.7 73.4 %collective-permute-start.14 = (bf16[256,1024]{1,0:T(8,128)(2,1)}, bf16[256,1024]{1,0:T(8,128)(2,1)}, u32[]{:S(2)}, u32[]{:S(2)}) collective-permute-start(bf16[256,1024]{1,0:T(8,128)(2,1)} %get-tuple-element.91), channel_id=1, source_target_pairs={{0,1},{1,0},{2,3},{3,2},{4,5},{5,4},{6,7},{7,6},{8,9},{9,8},{10,11... | collective-permute-start | bytes 1572872 | tf_op jit(solution)/shard_map/ppermute | solution.py:54
  243.8 45.9 %collective-permute-start.17 = (bf16[256,1024]{1,0:T(8,128)(2,1)}, bf16[256,1024]{1,0:T(8,128)(2,1)}, u32[]{:S(2)}, u32[]{:S(2)}) collective-permute-start(bf16[256,1024]{1,0:T(8,128)(2,1)} %fusion.7), channel_id=1, source_target_pairs={{0,2},{1,3},{8,10},{9,11},{16,18},{17,19},{24,26},{25,27}} | collective-permute-start | bytes 1572872 | tf_op jit(solution)/shard_map/ppermute | solution.py:61
  246.7 60.0 %collective-permute-start.62 = (bf16[4,8,128,128]{3,2,1,0:T(8,128)(2,1)S(1)}, bf16[4,8,128,128]{3,2,1,0:T(8,128)(2,1)S(1)}, u32[]{:S(2)}, u32[]{:S(2)}) collective-permute-start(bf16[4,8,128,128]{3,2,1,0:T(8,128)(2,1)S(1)} %copy-done.21), channel_id=1, source_target_pairs={{0,16},{8,24},{16,0},{24,8},{1,17},{9,25},{17,1},{25,9},{2,18},{10... | collective-permute-start | bytes 3145736 | tf_op jit(solution)/shard_map/ppermute | solution.py:78
  316.5 37.3 %collective-permute-start.64 = (bf16[4,8,128,128]{3,2,1,0:T(8,128)(2,1)}, bf16[4,8,128,128]{3,2,1,0:T(8,128)(2,1)S(1)}, u32[]{:S(2)}, u32[]{:S(2)}) collective-permute-start(bf16[4,8,128,128]{3,2,1,0:T(8,128)(2,1)} %get-tuple-element.61), channel_id=1, source_target_pairs={{0,16},{8,24},{16,0},{24,8},{1,17},{9,25},{17,1},{25,9},{2,18},{10... | collective-permute-start | bytes 3145736 | tf_op jit(solution)/shard_map/ppermute | solution.py:78
  320.1 37.6 %collective-permute-start.20 = (bf16[256,1024]{1,0:T(8,128)(2,1)S(1)}, bf16[256,1024]{1,0:T(8,128)(2,1)S(1)}, u32[]{:S(2)}, u32[]{:S(2)}) collective-permute-start(bf16[256,1024]{1,0:T(8,128)(2,1)S(1)} %get-tuple-element.83), channel_id=1, source_target_pairs={{6,4},{7,5},{14,12},{15,13},{22,20},{23,21},{30,28},{31,29}} | collective-permute-start | bytes 1572872 | tf_op jit(solution)/shard_map/ppermute | solution.py:62
  323.3 35.3 %collective-permute-start.45 = (bf16[256,1024]{1,0:T(8,128)(2,1)}, bf16[256,1024]{1,0:T(8,128)(2,1)}, u32[]{:S(2)}, u32[]{:S(2)}) collective-permute-start(bf16[256,1024]{1,0:T(8,128)(2,1)} %get-tuple-element.87), channel_id=1, source_target_pairs={{0,1},{1,0},{2,3},{3,2},{4,5},{5,4},{6,7},{7,6},{8,9},{9,8},{10,11... | collective-permute-start | bytes 1572872 | tf_op jit(solution)/shard_map/ppermute | solution.py:54
  335.0 35.5 %collective-permute-start.57 = (bf16[4,8,128,128]{3,2,1,0:T(8,128)(2,1)}, bf16[4,8,128,128]{3,2,1,0:T(8,128)(2,1)}, u32[]{:S(2)}, u32[]{:S(2)}) collective-permute-start(bf16[4,8,128,128]{3,2,1,0:T(8,128)(2,1)} %get-tuple-element.77), channel_id=1, source_target_pairs={{0,8},{8,0},{16,24},{24,16},{1,9},{9,1},{17,25},{25,17},{2,10},{10... | collective-permute-start | bytes 3145736 | tf_op jit(solution)/shard_map/ppermute | solution.py:71
  335.0 41.4 %collective-permute-start.58 = (bf16[4,8,128,128]{3,2,1,0:T(8,128)(2,1)}, bf16[4,8,128,128]{3,2,1,0:T(8,128)(2,1)}, u32[]{:S(2)}, u32[]{:S(2)}) collective-permute-start(bf16[4,8,128,128]{3,2,1,0:T(8,128)(2,1)} %get-tuple-element.58), channel_id=1, source_target_pairs={{0,16},{8,24},{16,0},{24,8},{1,17},{9,25},{17,1},{25,9},{2,18},{10... | collective-permute-start | bytes 3145736 | tf_op jit(solution)/shard_map/ppermute | solution.py:78
  358.6 40.2 %collective-permute-start.66 = (bf16[4,8,128,128]{3,2,1,0:T(8,128)(2,1)}, bf16[4,8,128,128]{3,2,1,0:T(8,128)(2,1)S(1)}, u32[]{:S(2)}, u32[]{:S(2)}) collective-permute-start(bf16[4,8,128,128]{3,2,1,0:T(8,128)(2,1)} %get-tuple-element.62), channel_id=1, source_target_pairs={{0,16},{8,24},{16,0},{24,8},{1,17},{9,25},{17,1},{25,9},{2,18},{10... | collective-permute-start | bytes 3145736 | tf_op jit(solution)/shard_map/ppermute | solution.py:78
  366.4 34.2 %collective-permute-start.21 = (bf16[256,1024]{1,0:T(8,128)(2,1)}, bf16[256,1024]{1,0:T(8,128)(2,1)}, u32[]{:S(2)}, u32[]{:S(2)}) collective-permute-start(bf16[256,1024]{1,0:T(8,128)(2,1)} %add_convert_fusion.13), channel_id=1, source_target_pairs={{4,2},{5,3},{6,4},{7,5},{12,10},{13,11},{14,12},{15,13},{20,18},{2... | collective-permute-start | bytes 1572872 | tf_op jit(solution)/shard_map/ppermute | solution.py:62
  370.5 50.8 %collective-permute-start.60 = (bf16[4,8,128,128]{3,2,1,0:T(8,128)(2,1)}, bf16[4,8,128,128]{3,2,1,0:T(8,128)(2,1)}, u32[]{:S(2)}, u32[]{:S(2)}) collective-permute-start(bf16[4,8,128,128]{3,2,1,0:T(8,128)(2,1)} %get-tuple-element.59), channel_id=1, source_target_pairs={{0,16},{8,24},{16,0},{24,8},{1,17},{9,25},{17,1},{25,9},{2,18},{10... | collective-permute-start | bytes 3145736 | tf_op jit(solution)/shard_map/ppermute | solution.py:78
  400.6 42.7 %collective-permute-start.68 = (bf16[4,8,128,128]{3,2,1,0:T(8,128)(2,1)}, bf16[4,8,128,128]{3,2,1,0:T(8,128)(2,1)S(1)}, u32[]{:S(2)}, u32[]{:S(2)}) collective-permute-start(bf16[4,8,128,128]{3,2,1,0:T(8,128)(2,1)} %get-tuple-element.63), channel_id=1, source_target_pairs={{0,16},{8,24},{16,0},{24,8},{1,17},{9,25},{17,1},{25,9},{2,18},{10... | collective-permute-start | bytes 3145736 | tf_op jit(solution)/shard_map/ppermute | solution.py:78
  403.5 44.3 %collective-permute-start.13 = (bf16[256,1024]{1,0:T(8,128)(2,1)}, bf16[256,1024]{1,0:T(8,128)(2,1)S(1)}, u32[]{:S(2)}, u32[]{:S(2)}) collective-permute-start(bf16[256,1024]{1,0:T(8,128)(2,1)} %get-tuple-element.88), channel_id=1, source_target_pairs={{0,1},{1,0},{2,3},{3,2},{4,5},{5,4},{6,7},{7,6},{8,9},{9,8},{10,11... | collective-permute-start | bytes 1572872 | tf_op jit(solution)/shard_map/ppermute | solution.py:54
  406.7 42.6 %collective-permute-start.19 = (bf16[256,1024]{1,0:T(8,128)(2,1)}, bf16[256,1024]{1,0:T(8,128)(2,1)S(1)}, u32[]{:S(2)}, u32[]{:S(2)}) collective-permute-start(bf16[256,1024]{1,0:T(8,128)(2,1)} %get-tuple-element.82), channel_id=1, source_target_pairs={{0,2},{1,3},{2,4},{3,5},{4,6},{5,7},{8,10},{9,11},{10,12},{11,13},... | collective-permute-start | bytes 1572872 | tf_op jit(solution)/shard_map/ppermute | solution.py:61
  (78 other events, 1688.0 us)

commit v2 on v0

v2 whole, which is shorter than its diff:
```python
import functools
import math

import jax
import jax.numpy as jnp
from jax import lax
from jax.experimental import pallas as pl
from jax.experimental.pallas import tpu as pltpu
from jax.sharding import PartitionSpec as P

gelu_scale = 0.7978845608028654
gelu_cube = 0.044715
BF = jnp.bfloat16
F32 = jnp.float32
ANY = pl.BlockSpec(memory_space=pl.ANY)
VMEM_BYTES = 56 * 1024 * 1024
small_cost = pl.CostEstimate(flops=1000, bytes_accessed=1000, transcendentals=0)


def gelu_pair(value):
    inner = gelu_scale * (value + gelu_cube * value * value * value)
    tangent = jnp.tanh(inner)
    result = 0.5 * value * (1.0 + tangent)
    slope = 0.5 * (1.0 + tangent) + 0.5 * value * (1.0 - tangent * tangent) * gelu_scale * (
        1.0 + 3.0 * gelu_cube * value * value
    )
    return (result, slope)


def line_pairs(line, step, first, last):
    return [
        (a * 2 + s, (a + step) * 2 + s)
        for a in range(first, last + 1)
        for s in range(2)
        if 0 <= a + step < line
    ]


def swap_pairs(first, last):
    return [(a * 2 + s, a * 2 + 1 - s) for a in range(first, last + 1) for s in range(2)]


def tie(value, others):
    return lax.optimization_barrier((value, others)) if others else (value, others)


def gather_parts(own, line):
    middle = line // 2
    held = {0: (own, own)}
    parts = [(own, 0, 0, 0, line - 1)]
    crossed, places, later = [], [], []
    for step in range(1, line + 1):
        k = step - 1
        (from_up, from_down), crossed = tie(held[k], crossed)
        for n, got in zip(places, crossed):
            parts[n] = (got,) + parts[n][1:]
        places = []
        if step < line:
            up = lax.ppermute(from_up, "tensor", line_pairs(line, 1, k, line - 2))
            down = lax.ppermute(from_down, "tensor", line_pairs(line, -1, 1, line - 1 - k))
            held[step] = (up, down)
            parts += [(up, -step, 0, step, line - 1), (down, step, 0, 0, line - 1 - step)]
        if k == 0:
            moves, after = [(own, 0, 0, line - 1)], []
        else:
            moves = [
                (from_down, k, 0, min(middle - 1, line - 1 - k)),
                (from_up, -k, max(middle, k), line - 1),
            ]
            after = [(from_up, -k, k, middle - 1), (from_down, k, middle, line - 1 - k)]
        crossed = []
        for value, d, first, last in moves + later:
            if first <= last:
                got = lax.ppermute(value, "tensor", swap_pairs(first, last))
                places.append(len(parts))
                parts.append((got, d, 1, first, last))
                crossed.append(got)
        later = after
    for value, d, first, last in later:
        if first <= last:
            got = lax.ppermute(value, "tensor", swap_pairs(first, last))
            parts.append((got, d, 1, first, last))
    return parts


class Order:
    def __init__(self, last):
        self.last = [last]

    def kernel(self, call, *args, also=()):
        out = call([*self.last, *also], *args)
        self.last = [jax.tree.leaves(out)[0]]
        return out


    def fusion(self, call, *args):
        args, before = tie(args, self.last)
        out = call(*args)
        self.last = [jax.tree.leaves(out)[0], *before]
        return out


def far_first(line):
    return sorted(range(line), key=lambda k: (-max(k, line - k) if k else 0, -k))


class LineSum:
    def __init__(self, keep, send):
        self.line, self.keep, self.k = keep.shape[0], keep, keep.shape[0] - 1
        self.got = [lax.ppermute(part, "tensor", swap_pairs(0, self.line - 1)) for part in send]
        self.moved = []

    def across(self, k):
        n = far_first(self.line).index(k)
        return self.got[2 * n // self.line], n % (self.line // 2)

    def step(self, order):
        k, line = self.k, self.line

        def both(k, keep, got):
            return keep[k].astype(F32) + got[self.across(k)[1]].astype(F32)

        if k > 0:

            def loads(keep, got_up, got_down, *moved):
                out = [both(k, keep, got_up), both(line - k, keep, got_down)]
                if moved:
                    out = [a + b.astype(F32) for a, b in zip(out, moved)]
                return [a.astype(BF) for a in out]

            got = self.across(k)[0], self.across(line - k)[0]
            up, down = order.fusion(loads, self.keep, *got, *self.moved)
            self.moved = [
                lax.ppermute(up, "tensor", line_pairs(line, 1, 0, line - 1 - k)),
                lax.ppermute(down, "tensor", line_pairs(line, -1, k, line - 1)),
            ]
        else:

            def last(keep, got, *moved):
                total = both(0, keep, got)
                for a in moved:
                    total = total + a.astype(F32)
                return total.astype(BF)

            self.total = order.fusion(last, self.keep, self.across(0)[0], *self.moved)
        self.k -= 1

    def finished(self):
        return self.k < 0


def core_swap(value):
    count = lax.axis_size("dp")
    return lax.ppermute(value, "dp", [(i, i ^ 1) for i in range(count)])


def ring_parts(value):
    count = lax.axis_size("dp")
    parts = [value]
    for t in range(2, count, 2):
        parts.append(lax.ppermute(value, "dp", [(i, (i + t) % count) for i in range(count)]))
    if len(parts) > 2:
        ring = lax.axis_index("dp") // 2
        stacked = jnp.stack(parts)
        parts = [
            lax.dynamic_index_in_dim(stacked, (ring - y) % len(parts), keepdims=False)
            for y in range(len(parts))
        ]
    return parts


def load_parts(meta, which, ranges, refs, full, sem):
    at, side = meta[0], meta[1]
    for (offset, other, first, last), ref in zip(ranges, refs):

        @pl.when((at >= first) & (at <= last))
        def _(offset=offset, other=other, ref=ref):
            slot = (at + offset) * 2 + (1 - side if other else side)
            pltpu.make_async_copy(ref.at[which], full.at[slot], sem).start()


def wait_parts(full, sem):
    pltpu.make_async_copy(full, full, sem).wait()


def block_at(pat, row, j, blocks, own_blocks, size):
    block = pat[row * blocks + j]
    return block // own_blocks, pl.ds(pl.multiple_of((block % own_blocks) * size, size), size)


def pick(full, pat, row, blocks, size):
    own_blocks = full.shape[-1] // size
    pieces = []
    for j in range(blocks):
        shard, lanes = block_at(pat, row, j, blocks, own_blocks, size)
        pieces.append(full[shard, :, lanes])
    return jnp.concatenate(pieces, axis=1)


def forward_kernel(ranges, meta, pat, *refs):
    parts, refs = refs[: len(ranges)], refs[len(ranges) :]
    w_ref, act_ref, slope_ref, full, sem = refs
    row = pl.program_id(0)

    @pl.when(row == 0)
    def _():
        load_parts(meta, 0, ranges, parts, full, sem)
        wait_parts(full, sem)

    together, blocks, size, _ = w_ref.shape
    for i in range(together):
        picked = pick(full, pat, row * together + i, blocks, size)
        pre = jnp.dot(picked, w_ref[i].reshape(blocks * size, size), preferred_element_type=F32)
        value, slope = gelu_pair(pre)
        act_ref[i] = value.astype(BF)
        slope_ref[i] = slope


def forward(meta, pat, parts, weights, line):
    rows, blocks, size, _ = weights.shape
    parts, ranges = [p[0] for p in parts], [p[1:] for p in parts]
    _, tok, width = parts[0].shape
    shards = 2 * line
    together = math.gcd(rows, 8)
    spec = pl.BlockSpec((together, tok, size), lambda r, *_: (r, 0, 0))
    return pl.pallas_call(
        functools.partial(forward_kernel, ranges),
        grid_spec=pltpu.PrefetchScalarGridSpec(
            num_scalar_prefetch=2,
            grid=(rows // together,),
            in_specs=[ANY] * len(parts)
            + [pl.BlockSpec((together, blocks, size, size), lambda r, *_: (r, 0, 0, 0))],
            out_specs=[spec, spec],
            scratch_shapes=[pltpu.VMEM((shards, tok, width), BF), pltpu.SemaphoreType.DMA],
        ),
        out_shape=[
            jax.ShapeDtypeStruct((rows, tok, size), BF),
            jax.ShapeDtypeStruct((rows, tok, size), F32),
        ],
        compiler_params=pltpu.CompilerParams(vmem_limit_bytes=VMEM_BYTES),
        cost_estimate=small_cost,
        name="forward_rows",
    )(meta, pat, *parts, weights)


def spread_kernel(flip, n_after, line, meta, pat, *refs):
    in_ref, w_ref, *out_refs, acc = refs[n_after:]
    step = pl.program_id(0)
    together, blocks, size, _ = w_ref.shape
    own_blocks = acc.shape[-1] // size

    @pl.when(step == 0)
    def _():
        acc[...] = jnp.zeros_like(acc)

    for i in range(together):
        value = in_ref[i]
        if flip:
            weight = w_ref[i].reshape(blocks * size, size)
            terms = lax.dot_general(
                value, weight, (((1,), (1,)), ((), ())), preferred_element_type=F32
            )
        else:
            weight = jnp.concatenate([w_ref[i, j] for j in range(blocks)], axis=1)
            terms = jnp.dot(value, weight, preferred_element_type=F32)
        for j in range(blocks):
            shard, lanes = block_at(pat, step * together + i, j, blocks, own_blocks, size)
            acc[shard, :, lanes] += terms[:, j * size : (j + 1) * size]

    @pl.when(step == pl.num_programs(0) - 1)
    def _():
        keep_ref, *send_refs = out_refs
        at, side = meta[0], meta[1]
        for n, k in enumerate(far_first(line)):
            place = lax.rem(at + k, line) * 2
            keep_ref[k] = acc[place + side].astype(BF)
            send_refs[2 * n // line][n % (line // 2)] = acc[place + 1 - side].astype(BF)


def spread(flip, meta, pat, line, width, after, values, weights):
    rows, blocks, size, _ = weights.shape
    tok = values.shape[1]
    together = math.gcd(rows, 4)
    whole = (2 * line, tok, width)
    shapes = [(line, tok, width)] + [(line // 2, tok, width)] * 2
    return pl.pallas_call(
        functools.partial(spread_kernel, flip, len(after), line),
        grid_spec=pltpu.PrefetchScalarGridSpec(
            num_scalar_prefetch=2,
            grid=(rows // together,),
            in_specs=[
                *[ANY] * len(after),
                pl.BlockSpec((together, tok, size), lambda r, *_: (r, 0, 0)),
                pl.BlockSpec((together, blocks, size, size), lambda r, *_: (r, 0, 0, 0)),
            ],
            out_specs=[pl.BlockSpec(d, lambda r, *_, n=len(d): (0,) * n) for d in shapes],
            scratch_shapes=[pltpu.VMEM(whole, F32)],
        ),
        out_shape=[jax.ShapeDtypeStruct(d, BF) for d in shapes],
        compiler_params=pltpu.CompilerParams(vmem_limit_bytes=VMEM_BYTES),
        cost_estimate=small_cost,
        name="spread_back" if flip else "spread_out",
    )(meta, pat, *after, values, weights)


def chunk_row(start, half, meta, i, rows):
    core = meta[2] if half == 0 else 1 - meta[2]
    return core * (rows // 2) + start + i


def chunk_kernel(n_after, ranges, spans, start, half, rows, chained, meta, pat, *refs):
    refs = refs[n_after:]
    parts, refs = refs[: len(ranges)], refs[len(ranges) :]
    act_ref, slope_ref, w_ref = refs[:3]
    more, refs = (refs[3 : 3 + 2 * len(spans)], refs[3 + 2 * len(spans) :]) if half == 0 else ((), refs[3:])
    refs = refs[1:] if chained else refs
    *outs, pg_ref, g_full, x_full, g_sem, x_sem = refs
    step = pl.program_id(0)
    together, blocks, size, _ = w_ref.shape
    row = chunk_row(start, half, meta, step * together, rows)

    @pl.when(step == 0)
    def _():
        load_parts(meta, 1, ranges, parts, g_full, g_sem)
        load_parts(meta, 0, ranges, parts, x_full, x_sem)
        wait_parts(g_full, g_sem)

    def store(n, which, i, terms):
        for j, term in enumerate(terms):
            if half == 0:
                term = term.astype(F32) + more[2 * n + which][i, j].astype(F32)
                outs[n][which, i, j] = term.astype(BF)
            else:
                outs[2 * n + which][i, j] = term

    def work(n):
        for i in range(together):
            grads = pick(g_full, pat, row + i, blocks, size)
            second = lax.dot_general(
                act_ref[i], grads, (((0,), (0,)), ((), ())), preferred_element_type=F32
            ).astype(BF)
            store(n, 0, i, [second[:, j * size : (j + 1) * size] for j in range(blocks)])
            weight = jnp.concatenate([w_ref[i, j] for j in range(blocks)], axis=1)
            act_grad = lax.dot_general(
                grads, weight, (((1,), (1,)), ((), ())), preferred_element_type=F32
            )
            pg_ref[i] = (act_grad * slope_ref[i]).astype(BF)
        if n == 0:

            @pl.when(step == 0)
            def _():
                wait_parts(x_full, x_sem)

        for i in range(together):
            picked = pick(x_full, pat, row + i, blocks, size)
            first = lax.dot_general(
                picked, pg_ref[i], (((0,), (0,)), ((), ())), preferred_element_type=F32
            ).astype(BF)
            store(n, 1, i, [first[j * size : (j + 1) * size] for j in range(blocks)])

    if len(spans) == 1:
        return work(0)
    for n, (low, count) in enumerate(spans):
        inside = (step >= low // together) & (step < (low + count) // together)
        pl.when(inside)(functools.partial(work, n))


def chunk(meta, pat, parts, act, slope, weights, line, start, counts, half, after, more, pg):
    rows, blocks, size, _ = weights.shape
    parts, ranges = [p[0] for p in parts], [p[1:] for p in parts]
    _, tok, width = parts[0].shape
    spans = [(sum(counts[:n]), count) for n, count in enumerate(counts)]
    together = math.gcd(start, rows // 2, 4, *counts)

    def at_row(r, meta, pat):
        return (chunk_row(start, half, meta, r * together, rows) // together, 0, 0)

    def in_span(low, count, lead):
        def index(r, *_):
            return lead + (jnp.clip(r - low // together, 0, count // together - 1), 0, 0, 0)

        return pl.BlockSpec((2,) * len(lead) + (together, blocks, size, size), index)

    row_spec = pl.BlockSpec((together, tok, size), at_row)
    w_spec = pl.BlockSpec((together, blocks, size, size), lambda r, m, p: at_row(r, m, p) + (0,))
    args = [*after, *parts, act, slope, weights]
    specs = [ANY] * (len(after) + len(parts)) + [row_spec, row_spec, w_spec]
    out_specs, out_shape = [], []
    for low, count in spans:
        if half == 0:
            specs += [in_span(low, count, ())] * 2
            out_specs.append(in_span(low, count, (0,)))
            out_shape.append(jax.ShapeDtypeStruct((2, count, blocks, size, size), BF))
        else:
            out_specs += [in_span(low, count, ())] * 2
            out_shape += [jax.ShapeDtypeStruct((count, blocks, size, size), BF)] * 2
    if half == 0:
        args += more
    aliases = {}
    if pg is not None:
        aliases = {2 + len(args): len(out_shape)}
        args.append(pg)
        specs.append(ANY)
    full = pltpu.VMEM((2 * line, tok, width), BF)
    *outs, pg = pl.pallas_call(
        functools.partial(
            chunk_kernel, len(after), ranges, spans, start, half, rows, pg is not None
        ),
        grid_spec=pltpu.PrefetchScalarGridSpec(
            num_scalar_prefetch=2,
            grid=(sum(counts) // together,),
            in_specs=specs,
            out_specs=out_specs + [row_spec],
            scratch_shapes=[full, full, pltpu.SemaphoreType.DMA, pltpu.SemaphoreType.DMA],
        ),
        out_shape=out_shape + [jax.ShapeDtypeStruct((rows, tok, size), BF)],
        input_output_aliases=aliases,
        compiler_params=pltpu.CompilerParams(vmem_limit_bytes=VMEM_BYTES),
        cost_estimate=small_cost,
        name="grad_rows",
    )(meta, pat, *args)
    return outs, pg


def place_kernel(n_after, total, chained, meta, *refs):
    refs = refs[n_after:]
    in_refs, refs = refs[:total], refs[total + (2 if chained else 0) + 1 :]
    for which in range(2):
        if len(refs) == 2:
            value = in_refs[which][...]
        else:
            value = in_refs[0][which].astype(F32)
            for ref in in_refs[1:]:
                value = value + ref[which].astype(F32)
            value = value.astype(BF)
            refs[2 + which][...] = value
        refs[which][...] = value


def place(meta, shape, start, half, after, parts, into):
    rows, blocks, size, _ = shape
    adding = half == 0
    count = parts[0].shape[1 if adding else 0]
    together = math.gcd(count, start, 2, rows // 2)
    n = len(parts)

    def at_row(r, meta):
        return (chunk_row(start, half, meta, r * together, rows) // together, 0, 0, 0)

    pair_spec = pl.BlockSpec((2, together, blocks, size, size), lambda r, *_: (0, r, 0, 0, 0))
    one_spec = pl.BlockSpec((together, blocks, size, size), lambda r, *_: (r, 0, 0, 0))
    out_spec = pl.BlockSpec((together, blocks, size, size), at_row)
    out_shape = [jax.ShapeDtypeStruct((8, 128), jnp.int32)] + [jax.ShapeDtypeStruct(shape, BF)] * 2
    out_specs = [ANY, out_spec, out_spec]
    if adding:
        out_shape += [jax.ShapeDtypeStruct(parts[0].shape[1:], BF)] * 2
        out_specs += [one_spec, one_spec]
    args = [*after, *parts]
    specs = [ANY] * len(after) + [pair_spec if adding else one_spec] * n
    aliases = {}
    if into is not None:
        aliases = {1 + len(args): 1, 2 + len(args): 2}
        args += into
        specs += [ANY, ANY]
    _, second, first, *own = pl.pallas_call(
        functools.partial(place_kernel, len(after), n, into is not None),
        grid_spec=pltpu.PrefetchScalarGridSpec(
            num_scalar_prefetch=1,
            grid=(count // together,),
            in_specs=specs,
            out_specs=out_specs,
        ),
        out_shape=out_shape,
        input_output_aliases=aliases,
        compiler_params=pltpu.CompilerParams(vmem_limit_bytes=VMEM_BYTES),
        cost_estimate=small_cost,
        name="place_rows",
    )(meta, *args)
    return _, [second, first], own


def chunk_counts(half_rows):
    unit = half_rows // 8
    if unit and half_rows == 8 * unit:
        return [unit, 4 * unit, 2 * unit, unit]
    return [1] * half_rows


def shards(tokens, pattern, first_blocks, second_blocks, out_grad):
    rows, blocks, size, _ = first_blocks.shape
    width = tokens.shape[1]
    line = lax.axis_size("tensor") // 2
    where = lax.axis_index("tensor")
    core = lax.axis_index("dp") % 2
    meta = jnp.stack([where // 2, where % 2, core]).astype(jnp.int32)
    pat = pattern.reshape(-1)

    half_rows = rows // 2
    counts = chunk_counts(half_rows)
    starts = [sum(counts[:n]) for n in range(len(counts))]
    chunks = range(len(counts))

    parts = gather_parts(jnp.stack([tokens, out_grad]), line)
    act, slope = forward(meta, pat, parts, first_blocks, line)
    order = Order(act)

    def grad_rows(first, last, half, more, pg):
        run = functools.partial(
            chunk, meta, pat, parts, act, slope, second_blocks, line, starts[first],
            counts[first:last], half,
        )
        return order.kernel(run, more, pg)

    def sum_half(first, last, pg):
        outs, pg = grad_rows(first, last, 0, [s for pair in sent[first:last] for s in pair], pg)
        if first > 0:
            outs[0], kept[0][1:] = tie(outs[0], kept[0][1:])
        return [ring_parts(grads) for grads in outs], pg

    def other_half(first, last, pg):
        outs, pg = grad_rows(first, last, 1, None, pg)
        swapped = [core_swap(grads) for grads in outs]
        return [swapped[n : n + 2] for n in range(0, len(swapped), 2)], pg

    last = len(counts)
    sent, pg = other_half(0, last, None)
    kept, pg = sum_half(0, 1, pg)
    if last > 1:
        more, pg = sum_half(1, last, pg)
        kept += more

    totals, own = None, {}

    def settle(n, totals, also=()):
        run = functools.partial(place, meta, first_blocks.shape, starts[n], 0)
        _, totals, one = order.kernel(run, kept[n], totals, also=also)
        own[n] = [core_swap(v) for v in one]
        return totals

    def settle_other(n, totals):
        run = functools.partial(place, meta, first_blocks.shape, starts[n], 1)
        return order.kernel(run, own[n], totals)[1]

    totals = settle(0, totals)
    sums = []
    for flip, values, weights in ((False, act, second_blocks), (True, pg, first_blocks)):
        run = functools.partial(spread, flip, meta, pat, line, width)
        keep, *send = order.kernel(run, values, weights)
        sums.append(LineSum(keep, send))
    out, back = sums
    while out.k > 0:
        out.step(order)
    back.step(order)
    for n in range(1, last):
        totals = settle(n, totals)
        totals = settle_other(n - 1, totals)
        for item in (out, back, back):
            if not item.finished():
                item.step(order)
    for item in (out, back):
        while not item.finished():
            item.step(order)
    totals = settle_other(last - 1, totals)
    return (out.total, back.total, totals[1], totals[0])


def solution(mesh):
    placed = (
        P("dp", "tensor"),
        P("tensor", None),
        P("tensor", None, None, None),
        P("tensor", None, None, None),
        P("dp", "tensor"),
    )
    return jax.shard_map(
        shards,
        mesh=mesh,
        in_specs=placed,
        out_specs=(
            P("dp", "tensor"),
            P("dp", "tensor"),
            P("tensor", None, None, None),
            P("tensor", None, None, None),
        ),
        check_vma=False,
    )
```

time: 786 us -> 380 us (0.48); the launches traced: 775 us -> 379 us
  waiting for transfers between devices: 441 us -> 153 us
  matrix products: 196 us -> 0 us
  Pallas kernels: 0 us -> 125 us
  local copies, waits for them, and re-layouts: 122 us -> 7.99 us
  starting transfers between devices: 0.21 us -> 79 us
  between operations: 14.3 us -> 1.31 us
  other arithmetic: 0.7 us -> 12.4 us
    dot_general x8 -> x0, matrix products: 196 us -> none  [the longest x2 109 us: place_blocks(): jnp.einsum('trkc,rkf->ftc', terms, select, precision=lax.Precision.HIGHEST)]
    unnamed x7 -> x0, waiting for transfers between devices: 169 us -> none
    ppermute x0 -> x51, waiting for transfers between devices: none -> 153 us  [the longest x3 45.6 us: gather_parts(): lax.ppermute(from_down, 'tensor', line_pairs(line, -1, 1, line - 1 - k))]
    all_gather x2 -> x0, waiting for transfers between devices: 143 us -> none  [the longest x1 74.5 us: shards(): lax.all_gather(tokens, 'tensor', axis=1, tiled=True)]
    psum x1 -> x0, waiting for transfers between devices: 130 us -> none  [shards(): lax.psum(first_term.astype(jnp.bfloat16), 'dp').astype(jnp.float32)]
    pallas_call x0 -> x14, Pallas kernels: none -> 125 us  [the longest x3 43.9 us: chunk(): pl.pallas_call(functools.partial(chunk_kernel, len(after), ranges, spans,...]
    ppermute x0 -> x51, starting transfers between devices: none -> 79 us  [the longest x6 31.5 us: step(): lax.ppermute(up, 'tensor', line_pairs(line, 1, 0, line - 1 - k))]
    gather x4 -> x0, local copies, waits for them, and re-layouts: 69 us -> none  [the longest x2 34.5 us: shards(): picked = full_tokens[:, pattern, :]]
  transfers between devices with their start and end apart: 5 -> 51, of which waited for: 5 -> 17; matrix products, arithmetic and copies ran while one was open for 23% -> 3% of each run, Pallas kernels for 0% -> 24%
where the time goes in v2:
time: 380 us; the launch traced here: 379 us
  waiting for transfers between devices  153 us (40%)
  Pallas kernels  125 us (33%)
  starting transfers between devices  79 us (21%)
  other arithmetic  12.4 us (3%)
  local copies, waits for them, and re-layouts  7.99 us (2%)
    ppermute x3, waiting for transfers between devices, gather_parts(): lax.ppermute(from_down, 'tensor', line_pairs(line, -1, 1, line - 1 - k))  45.6 us
    pallas_call x3, Pallas kernels, chunk(): pl.pallas_call(functools.partial(chunk_kernel, len(after), ranges, spans,...  43.9 us
    ppermute x4, waiting for transfers between devices, __init__(): lax.ppermute(part, 'tensor', swap_pairs(0, self.line - 1))  35.8 us
    pallas_call x8, Pallas kernels, place(): pl.pallas_call(functools.partial(place_kernel, len(after), n, into is not...  34.2 us
    pallas_call x2, Pallas kernels, spread(): pl.pallas_call(functools.partial(spread_kernel, flip, len(after), line),...  32.2 us
    ppermute x6, starting transfers between devices, step(): lax.ppermute(up, 'tensor', line_pairs(line, 1, 0, line - 1 - k))  31.5 us
    ppermute x6, waiting for transfers between devices, step(): lax.ppermute(up, 'tensor', line_pairs(line, 1, 0, line - 1 - k))  21 us
    ppermute x3, waiting for transfers between devices, gather_parts(): up = lax.ppermute(from_up, 'tensor', line_pairs(line, 1, k, line - 2))  19.5 us
  transfers between devices with their start and end apart: 51, of which 17 were waited for; matrix products, arithmetic and copies ran while one was open for 3% of the time, Pallas kernels for 24%

profile of v2, /device:TPU:0, one launch (start us, length us, event | category | flops | bytes accessed | tf_op | source)
XLA Modules:
  0.0 378.6 jit_solution(18250492909261632620)
XLA Ops:
  2.0 5.0 %collective-permute-start = (bf16[2,256,1024]{2,1,0:T(8,128)(2,1)S(1)}, bf16[2,256,1024]{2,1,0:T(8,128)(2,1)S(1)}, u32[]{:S(2)}, u32[]{:S(2)}) collective-permute-start(bf16[2,256,1024]{2,1,0:T(8,128)(2,1)S(1)} %pad_maximum_fusion.refs_0_.refs_1_), channel_id=1, source_target_pairs={{0,2},{1,3},{2,4},{3,5},{4,6},{5,7},{8,10},{9,11},{10,12},{11,13},... | collective-permute-start | bytes 3145736 | tf_op jit(solution)/shard_map/ppermute | solution.py:59
  9.8 19.5 %collective-permute-done.refs_1_.refs_2_ = bf16[2,256,1024]{2,1,0:T(8,128)(2,1)S(1)} collective-permute-done((bf16[2,256,1024]{2,1,0:T(8,128)(2,1)S(1)}, bf16[2,256,1024]{2,1,0:T(8,128)(2,1)S(1)}, u32[]{:S(2)}, u32[]{:S(2)}) %collective-permute-start) | collective-permute-done | bytes 1048608 | tf_op jit(solution)/shard_map/ppermute | solution.py:59
  41.1 21.0 %collective-permute-done.4.refs_5_.refs_6_ = bf16[2,256,1024]{2,1,0:T(8,128)(2,1)S(1)} collective-permute-done((bf16[2,256,1024]{2,1,0:T(8,128)(2,1)S(1)}, bf16[2,256,1024]{2,1,0:T(8,128)(2,1)S(1)}, u32[]{:S(2)}, u32[]{:S(2)}) %collective-permute-start.4) | collective-permute-done | bytes 1048608 | tf_op jit(solution)/shard_map/ppermute | solution.py:60
  69.6 20.5 %collective-permute-done.8.refs_9_.refs_10_ = bf16[2,256,1024]{2,1,0:T(8,128)(2,1)} collective-permute-done((bf16[2,256,1024]{2,1,0:T(8,128)(2,1)S(1)}, bf16[2,256,1024]{2,1,0:T(8,128)(2,1)}, u32[]{:S(2)}, u32[]{:S(2)}) %collective-permute-start.8) | collective-permute-done | bytes 1048608 | tf_op jit(solution)/shard_map/ppermute | solution.py:60
  97.0 17.5 %collective-permute-done.13.refs_14_.refs_15_ = bf16[2,256,1024]{2,1,0:T(8,128)(2,1)} collective-permute-done((bf16[2,256,1024]{2,1,0:T(8,128)(2,1)}, bf16[2,256,1024]{2,1,0:T(8,128)(2,1)}, u32[]{:S(2)}, u32[]{:S(2)}) %collective-permute-start.13) | collective-permute-done | bytes 1048608 | tf_op jit(solution)/shard_map/ppermute | solution.py:74
  114.5 14.3 %forward_rows.1 = (bf16[32,256,128]{2,1,0:T(8,128)(2,1)}, f32[32,256,128]{2,1,0:T(8,128)}) custom-call(s32[3]{0:T(128)} %pad_add_fusion.meta, s32[256]{0:T(256)} %reshape.55.pat, bf16[2,256,1024]{2,1,0:T(8,128)(2,1)} %copy-done, bf16[2,256,1024]{2,1,0:T(8,128)(2,1)} %copy-done.1, bf16[2,256,1024]{2,1,0:T(8,128)(2,1)} %copy-done.2, ...), custom_call_target="tpu_custom_call" | custom-call | flops 1000 | bytes 1000 | tf_op jit(solution)/shard_map/forward_rows/pallas_call | solution.py:226
  128.9 18.2 %grad_rows.3 = (bf16[2,8,128,128]{3,2,1,0:T(8,128)(2,1)}, bf16[2,8,128,128]{3,2,1,0:T(8,128)(2,1)}, bf16[8,8,128,128]{3,2,1,0:T(8,128)(2,1)}, bf16[8,8,128,128]{...) custom-call(s32[3]{0:T(128)} %pad_add_fusion.meta, ...), custom_call_target="tpu_custom_call" | custom-call | flops 1000 | bytes 1000 | tf_op jit(solution)/shard_map/grad_rows/pallas_call | solution.py:405
  149.4 6.6 %collective-permute-done.16.refs_21_ = bf16[2,8,128,128]{3,2,1,0:T(8,128)(2,1)S(1)} collective-permute-done((bf16[2,8,128,128]{3,2,1,0:T(8,128)(2,1)}, bf16[2,8,128,128]{3,2,1,0:T(8,128)(2,1)S(1)}, u32[]{:S(2)}, u32[]{:S(2)}) %collective-permute-start.16) | collective-permute-done | bytes 524320 | tf_op jit(solution)/shard_map/ppermute | solution.py:154
  157.3 7.7 %grad_rows.4 = (bf16[2,2,8,128,128]{4,3,2,1,0:T(8,128)(2,1)}, bf16[32,256,128]{2,1,0:T(8,128)(2,1)}) custom-call(s32[3]{0:T(128)} %pad_add_fusion.meta, s32[256]{0:T(256)} %reshape.55.pat, bf16[2,8,128,128]{3,2,1,0:T(8,128)(2,1)} %get-tuple-element.139.refs_0_, bf16[2,256,1024]{2,1,0:T(8,128)(2,1)} %copy-done, ...), custom_call_target="tpu_custom_call", output_to_operand_aliasing={{1}: (24, {})} | custom-call | flops 1000 | bytes 1000 | tf_op jit(solution)/shard_map/grad_rows/pallas_call | solution.py:405
  170.0 18.1 %grad_rows.5 = (bf16[2,8,8,128,128]{4,3,2,1,0:T(8,128)(2,1)}, bf16[2,4,8,128,128]{4,3,2,1,0:T(8,128)(2,1)}, bf16[2,2,8,128,128]{4,3,2,1,0:T(8,128)(2,1)}, bf16[32,256,128]{2,1,0:T(8,128)(2,1)}) custom-call(s32[3]{0:T(128)} %pad_add_fusion.meta, s32[256]{0:T(256)} %reshape.55.pat, ...), custom_call_target="tpu_custom_call", output_to_operand_aliasing={{3}: (28, {})} | custom-call | flops 1000 | bytes 1000 | tf_op jit(solution)/shard_map/grad_rows/pallas_call | solution.py:405
  196.4 15.8 %spread_out.1 = (bf16[4,256,1024]{2,1,0:T(8,128)(2,1)}, bf16[2,256,1024]{2,1,0:T(8,128)(2,1)}, bf16[2,256,1024]{2,1,0:T(8,128)(2,1)}) custom-call(s32[3]{0:T(128)} %pad_add_fusion.meta, s32[256]{0:T(256)} %reshape.55.pat, s32[8,128]{1,0:T(8,128)} %get-tuple-element.152.refs_0_, bf16[32,256,128]{2,1,0:T(8,128)(2,1)} %get-tuple-element.137.refs_0_.refs_17_.refs_1_, ...), custom_call_target="tpu_custom_call" | custom-call | flops 1000 | bytes 1000 | tf_op jit(solution)/shard_map/spread_out/pallas_call | solution.py:286
  214.2 16.4 %spread_back.1 = (bf16[4,256,1024]{2,1,0:T(8,128)(2,1)}, bf16[2,256,1024]{2,1,0:T(8,128)(2,1)}, bf16[2,256,1024]{2,1,0:T(8,128)(2,1)}) custom-call(s32[3]{0:T(128)} %pad_add_fusion.meta, s32[256]{0:T(256)} %reshape.55.pat, bf16[4,256,1024]{2,1,0:T(8,128)(2,1)} %get-tuple-element.193.refs_0_, bf16[32,256,128]{2,1,0:T(8,128)(2,1)} %get-tuple-element.156.refs_1_, ...), custom_call_target="tpu_custom_call" | custom-call | flops 1000 | bytes 1000 | tf_op jit(solution)/shard_map/spread_back/pallas_call | solution.py:286
  230.6 7.8 %collective-permute-done.25 = bf16[2,256,1024]{2,1,0:T(8,128)(2,1)S(1)} collective-permute-done((bf16[2,256,1024]{2,1,0:T(8,128)(2,1)}, bf16[2,256,1024]{2,1,0:T(8,128)(2,1)S(1)}, u32[]{:S(2)}, u32[]{:S(2)}) %collective-permute-start.25) | collective-permute-done | bytes 1048608 | tf_op jit(solution)/shard_map/ppermute | solution.py:110
  238.9 4.7 %collective-permute-start.26 = (bf16[256,1024]{1,0:T(8,128)(2,1)S(1)}, bf16[256,1024]{1,0:T(8,128)(2,1)S(1)}, u32[]{:S(2)}, u32[]{:S(2)}) collective-permute-start(bf16[256,1024]{1,0:T(8,128)(2,1)S(1)} %get-tuple-element.182.refs_3_), channel_id=1, source_target_pairs={{0,2},{1,3},{8,10},{9,11},{16,18},{17,19},{24,26},{25,27}} | collective-permute-start | bytes 1572872 | tf_op jit(solution)/shard_map/ppermute | solution.py:134
  244.3 14.6 %collective-permute-done.24 = bf16[2,256,1024]{2,1,0:T(8,128)(2,1)S(1)} collective-permute-done((bf16[2,256,1024]{2,1,0:T(8,128)(2,1)}, bf16[2,256,1024]{2,1,0:T(8,128)(2,1)S(1)}, u32[]{:S(2)}, u32[]{:S(2)}) %collective-permute-start.24) | collective-permute-done | bytes 1048608 | tf_op jit(solution)/shard_map/ppermute | solution.py:110
  259.4 4.5 %collective-permute-start.28 = (bf16[256,1024]{1,0:T(8,128)(2,1)S(1)}, bf16[256,1024]{1,0:T(8,128)(2,1)S(1)}, u32[]{:S(2)}, u32[]{:S(2)}) collective-permute-start(bf16[256,1024]{1,0:T(8,128)(2,1)S(1)} %get-tuple-element.181.refs_2_), channel_id=1, source_target_pairs={{0,2},{1,3},{2,4},{3,5},{8,10},{9,11},{10,12},{11,13},{16,18},{17,... | collective-permute-start | bytes 1572872 | tf_op jit(solution)/shard_map/ppermute | solution.py:134
  266.8 6.6 %collective-permute-done.28 = bf16[256,1024]{1,0:T(8,128)(2,1)S(1)} collective-permute-done((bf16[256,1024]{1,0:T(8,128)(2,1)S(1)}, bf16[256,1024]{1,0:T(8,128)(2,1)S(1)}, u32[]{:S(2)}, u32[]{:S(2)}) %collective-permute-start.28) | collective-permute-done | bytes 524320 | tf_op jit(solution)/shard_map/ppermute | solution.py:134
  275.6 8.4 %collective-permute-start.30 = (bf16[256,1024]{1,0:T(8,128)(2,1)}, bf16[256,1024]{1,0:T(8,128)(2,1)}, u32[]{:S(2)}, u32[]{:S(2)}) collective-permute-start(bf16[256,1024]{1,0:T(8,128)(2,1)} %get-tuple-element.180.refs_1_), channel_id=1, source_target_pairs={{0,2},{1,3},{2,4},{3,5},{4,6},{5,7},{8,10},{9,11},{10,12},{11,13},... | collective-permute-start | bytes 1572872 | tf_op jit(solution)/shard_map/ppermute | solution.py:134
  284.1 6.0 %collective-permute-done.32 = bf16[2,256,1024]{2,1,0:T(8,128)(2,1)S(1)} collective-permute-done((bf16[2,256,1024]{2,1,0:T(8,128)(2,1)S(1)}, bf16[2,256,1024]{2,1,0:T(8,128)(2,1)S(1)}, u32[]{:S(2)}, u32[]{:S(2)}) %collective-permute-start.32) | collective-permute-done | bytes 1048608 | tf_op jit(solution)/shard_map/ppermute | solution.py:110
  294.1 8.0 %place_rows.9 = (s32[8,128]{1,0:T(8,128)}, bf16[32,8,128,128]{3,2,1,0:T(8,128)(2,1)}, bf16[32,8,128,128]{3,2,1,0:T(8,128)(2,1)}, bf16[8,8,128,128]{3,2,1,0:T(8,128)(2,1)}, bf16[8,8,128,128]{3,2,1,0:T(8,128)(2,1)}) custom-call(s32[3]{0:T(128)} %pad_add_fusion.meta, ...), custom_call_target="tpu_custom_call", output_to_operand_aliasing={{1}: (8, {}), {2}: (9, {})} | custom-call | flops 1000 | bytes 1000 | tf_op jit(solution)/shard_map/place_rows/pallas_call | solution.py:465
  302.2 7.3 %collective-permute-done.36 = bf16[2,256,1024]{2,1,0:T(8,128)(2,1)S(1)} collective-permute-done((bf16[2,256,1024]{2,1,0:T(8,128)(2,1)}, bf16[2,256,1024]{2,1,0:T(8,128)(2,1)S(1)}, u32[]{:S(2)}, u32[]{:S(2)}) %collective-permute-start.36) | collective-permute-done | bytes 1048608 | tf_op jit(solution)/shard_map/ppermute | solution.py:110
  330.9 10.3 %collective-permute-done.39 = bf16[256,1024]{1,0:T(8,128)(2,1)S(1)} collective-permute-done((bf16[256,1024]{1,0:T(8,128)(2,1)S(1)}, bf16[256,1024]{1,0:T(8,128)(2,1)S(1)}, u32[]{:S(2)}, u32[]{:S(2)}) %collective-permute-start.39) | collective-permute-done | bytes 524320 | tf_op jit(solution)/shard_map/ppermute | solution.py:134
  344.2 5.8 %collective-permute-start.41 = (bf16[256,1024]{1,0:T(8,128)(2,1)S(1)}, bf16[256,1024]{1,0:T(8,128)(2,1)S(1)}, u32[]{:S(2)}, u32[]{:S(2)}) collective-permute-start(bf16[256,1024]{1,0:T(8,128)(2,1)S(1)} %get-tuple-element.245.refs_0_), channel_id=1, source_target_pairs={{0,2},{1,3},{2,4},{3,5},{4,6},{5,7},{8,10},{9,11},{10,12},{11,13},... | collective-permute-start | bytes 1572872 | tf_op jit(solution)/shard_map/ppermute | solution.py:134
  356.4 5.4 %place_rows.12 = (s32[8,128]{1,0:T(8,128)}, bf16[32,8,128,128]{3,2,1,0:T(8,128)(2,1)}, bf16[32,8,128,128]{3,2,1,0:T(8,128)(2,1)}) custom-call(s32[3]{0:T(128)} %pad_add_fusion.meta, s32[8,128]{1,0:T(8,128)} %get-tuple-element.218.refs_0_, bf16[8,8,128,128]{3,2,1,0:T(8,128)(2,1)} %collective-permute-done.44.refs_1_, ...), custom_call_target="tpu_custom_call", output_to_operand_aliasing={{1}: (4, {}), {2}: (5, {})} | custom-call | flops 1000 | bytes 1000 | tf_op jit(solution)/shard_map/place_rows/pallas_call | solution.py:465
  (184 shorter events, 107.2 us)
Async XLA Ops:
  2.0 27.3 %collective-permute-start = (bf16[2,256,1024]{2,1,0:T(8,128)(2,1)S(1)}, bf16[2,256,1024]{2,1,0:T(8,128)(2,1)S(1)}, u32[]{:S(2)}, u32[]{:S(2)}) collective-permute-start(bf16[2,256,1024]{2,1,0:T(8,128)(2,1)S(1)} %pad_maximum_fusion.refs_0_.refs_1_), channel_id=1, source_target_pairs={{0,2},{1,3},{2,4},{3,5},{4,6},{5,7},{8,10},{9,11},{10,12},{11,13},... | collective-permute-start | bytes 3145736 | tf_op jit(solution)/shard_map/ppermute | solution.py:59
  7.0 26.5 %collective-permute-start.1 = (bf16[2,256,1024]{2,1,0:T(8,128)(2,1)S(1)}, bf16[2,256,1024]{2,1,0:T(8,128)(2,1)S(1)}, u32[]{:S(2)}, u32[]{:S(2)}) collective-permute-start(bf16[2,256,1024]{2,1,0:T(8,128)(2,1)S(1)} %pad_maximum_fusion.refs_0_.refs_1_), channel_id=1, source_target_pairs={{2,0},{3,1},{4,2},{5,3},{6,4},{7,5},{10,8},{11,9},{12,10},{13,11},... | collective-permute-start | bytes 3145736 | tf_op jit(solution)/shard_map/ppermute | solution.py:60
  8.3 25.2 %collective-permute-start.2 = (bf16[2,256,1024]{2,1,0:T(8,128)(2,1)S(1)}, bf16[2,256,1024]{2,1,0:T(8,128)(2,1)S(1)}, u32[]{:S(2)}, u32[]{:S(2)}) collective-permute-start(bf16[2,256,1024]{2,1,0:T(8,128)(2,1)S(1)} %pad_maximum_fusion.refs_0_.refs_1_), channel_id=1, source_target_pairs={{0,1},{1,0},{2,3},{3,2},{4,5},{5,4},{6,7},{7,6},{8,9},{9,8},{10,11... | collective-permute-start | bytes 3145736 | tf_op jit(solution)/shard_map/ppermute | solution.py:74
  34.2 27.9 %collective-permute-start.4 = (bf16[2,256,1024]{2,1,0:T(8,128)(2,1)S(1)}, bf16[2,256,1024]{2,1,0:T(8,128)(2,1)S(1)}, u32[]{:S(2)}, u32[]{:S(2)}) collective-permute-start(bf16[2,256,1024]{2,1,0:T(8,128)(2,1)S(1)} %collective-permute-done.1.refs_2_.refs_3_), channel_id=1, source_target_pairs={{2,0},{3,1},{4,2},{5,3},{10,8},{11,9},{12,10},{13,11},{18,16},{19,... | collective-permute-start | bytes 3145736 | tf_op jit(solution)/shard_map/ppermute | solution.py:60
  35.5 26.6 %collective-permute-start.5 = (bf16[2,256,1024]{2,1,0:T(8,128)(2,1)S(1)}, bf16[2,256,1024]{2,1,0:T(8,128)(2,1)S(1)}, u32[]{:S(2)}, u32[]{:S(2)}) collective-permute-start(bf16[2,256,1024]{2,1,0:T(8,128)(2,1)S(1)} %collective-permute-done.1.refs_2_.refs_3_), channel_id=1, source_target_pairs={{0,1},{1,0},{2,3},{3,2},{8,9},{9,8},{10,11},{11,10},{16,17},{17,16... | collective-permute-start | bytes 3145736 | tf_op jit(solution)/shard_map/ppermute | solution.py:74
  38.9 23.2 %collective-permute-start.6 = (bf16[2,256,1024]{2,1,0:T(8,128)(2,1)S(1)}, bf16[2,256,1024]{2,1,0:T(8,128)(2,1)S(1)}, u32[]{:S(2)}, u32[]{:S(2)}) collective-permute-start(bf16[2,256,1024]{2,1,0:T(8,128)(2,1)S(1)} %collective-permute-done.refs_1_.refs_2_), channel_id=1, source_target_pairs={{4,5},{5,4},{6,7},{7,6},{12,13},{13,12},{14,15},{15,14},{20,21},{2... | collective-permute-start | bytes 3145736 | tf_op jit(solution)/shard_map/ppermute | solution.py:74
  39.7 26.4 %collective-permute-start.11 = (bf16[2,256,1024]{2,1,0:T(8,128)(2,1)S(1)}, bf16[2,256,1024]{2,1,0:T(8,128)(2,1)S(1)}, u32[]{:S(2)}, u32[]{:S(2)}) collective-permute-start(bf16[2,256,1024]{2,1,0:T(8,128)(2,1)S(1)} %collective-permute-done.refs_1_.refs_2_), channel_id=1, source_target_pairs={{2,3},{3,2},{10,11},{11,10},{18,19},{19,18},{26,27},{27,26}} | collective-permute-start | bytes 3145736 | tf_op jit(solution)/shard_map/ppermute | solution.py:74
  40.4 29.1 %collective-permute-start.12 = (bf16[2,256,1024]{2,1,0:T(8,128)(2,1)S(1)}, bf16[2,256,1024]{2,1,0:T(8,128)(2,1)S(1)}, u32[]{:S(2)}, u32[]{:S(2)}) collective-permute-start(bf16[2,256,1024]{2,1,0:T(8,128)(2,1)S(1)} %collective-permute-done.1.refs_2_.refs_3_), channel_id=1, source_target_pairs={{4,5},{5,4},{12,13},{13,12},{20,21},{21,20},{28,29},{29,28}} | collective-permute-start | bytes 3145736 | tf_op jit(solution)/shard_map/ppermute | solution.py:74
  64.1 26.0 %collective-permute-start.10 = (bf16[2,256,1024]{2,1,0:T(8,128)(2,1)S(1)}, bf16[2,256,1024]{2,1,0:T(8,128)(2,1)S(1)}, u32[]{:S(2)}, u32[]{:S(2)}) collective-permute-start(bf16[2,256,1024]{2,1,0:T(8,128)(2,1)S(1)} %collective-permute-done.3.refs_4_.refs_5_), channel_id=1, source_target_pairs={{4,5},{5,4},{6,7},{7,6},{12,13},{13,12},{14,15},{15,14},{20,21},{2... | collective-permute-start | bytes 3145736 | tf_op jit(solution)/shard_map/ppermute | solution.py:74
  64.8 25.3 %collective-permute-start.8 = (bf16[2,256,1024]{2,1,0:T(8,128)(2,1)S(1)}, bf16[2,256,1024]{2,1,0:T(8,128)(2,1)}, u32[]{:S(2)}, u32[]{:S(2)}) collective-permute-start(bf16[2,256,1024]{2,1,0:T(8,128)(2,1)S(1)} %collective-permute-done.4.refs_5_.refs_6_), channel_id=1, source_target_pairs={{2,0},{3,1},{10,8},{11,9},{18,16},{19,17},{26,24},{27,25}} | collective-permute-start | bytes 3145736 | tf_op jit(solution)/shard_map/ppermute | solution.py:60
  66.1 24.4 %collective-permute-start.9 = (bf16[2,256,1024]{2,1,0:T(8,128)(2,1)S(1)}, bf16[2,256,1024]{2,1,0:T(8,128)(2,1)S(1)}, u32[]{:S(2)}, u32[]{:S(2)}) collective-permute-start(bf16[2,256,1024]{2,1,0:T(8,128)(2,1)S(1)} %collective-permute-done.4.refs_5_.refs_6_), channel_id=1, source_target_pairs={{0,1},{1,0},{2,3},{3,2},{8,9},{9,8},{10,11},{11,10},{16,17},{17,16... | collective-permute-start | bytes 3145736 | tf_op jit(solution)/shard_map/ppermute | solution.py:74
  90.6 23.9 %collective-permute-start.13 = (bf16[2,256,1024]{2,1,0:T(8,128)(2,1)}, bf16[2,256,1024]{2,1,0:T(8,128)(2,1)}, u32[]{:S(2)}, u32[]{:S(2)}) collective-permute-start(bf16[2,256,1024]{2,1,0:T(8,128)(2,1)} %collective-permute-done.8.refs_9_.refs_10_), channel_id=1, source_target_pairs={{0,1},{1,0},{8,9},{9,8},{16,17},{17,16},{24,25},{25,24}} | collective-permute-start | bytes 3145736 | tf_op jit(solution)/shard_map/ppermute | solution.py:74
  165.8 25.4 %collective-permute-start.23 = (bf16[2,2,8,128,128]{4,3,2,1,0:T(8,128)(2,1)}, bf16[2,2,8,128,128]{4,3,2,1,0:T(8,128)(2,1)S(1)}, u32[]{:S(2)}, u32[]{:S(2)}) collective-permute-start(bf16[2,2,8,128,128]{4,3,2,1,0:T(8,128)(2,1)} %get-tuple-element.142.refs_0_.refs_1_), channel_id=1, source_target_pairs={{0,16},{8,24},{16,0},{24,8},{1,17},{9,25},{17,1},{25,9},{2,18},{10... | collective-permute-start | bytes 3145736 | tf_op jit(solution)/shard_map/ppermute | solution.py:161
  191.2 100.2 %collective-permute-start.33 = (bf16[2,8,8,128,128]{4,3,2,1,0:T(8,128)(2,1)}, bf16[2,8,8,128,128]{4,3,2,1,0:T(8,128)(2,1)}, u32[]{:S(2)}, u32[]{:S(2)}) collective-permute-start(bf16[2,8,8,128,128]{4,3,2,1,0:T(8,128)(2,1)} %get-tuple-element.184.refs_0_.refs_5_), channel_id=1, source_target_pairs={{0,16},{8,24},{16,0},{24,8},{1,17},{9,25},{17,1},{25,9},{2,18},{10... | collective-permute-start | bytes 12582920 | tf_op jit(solution)/shard_map/ppermute | solution.py:161
  212.2 26.3 %collective-permute-start.25 = (bf16[2,256,1024]{2,1,0:T(8,128)(2,1)}, bf16[2,256,1024]{2,1,0:T(8,128)(2,1)S(1)}, u32[]{:S(2)}, u32[]{:S(2)}) collective-permute-start(bf16[2,256,1024]{2,1,0:T(8,128)(2,1)} %get-tuple-element.155), channel_id=1, source_target_pairs={{0,1},{1,0},{2,3},{3,2},{4,5},{5,4},{6,7},{7,6},{8,9},{9,8},{10,11... | collective-permute-start | bytes 3145736 | tf_op jit(solution)/shard_map/ppermute | solution.py:110
  213.7 45.2 %collective-permute-start.24 = (bf16[2,256,1024]{2,1,0:T(8,128)(2,1)}, bf16[2,256,1024]{2,1,0:T(8,128)(2,1)S(1)}, u32[]{:S(2)}, u32[]{:S(2)}) collective-permute-start(bf16[2,256,1024]{2,1,0:T(8,128)(2,1)} %get-tuple-element.154), channel_id=1, source_target_pairs={{0,1},{1,0},{2,3},{3,2},{4,5},{5,4},{6,7},{7,6},{8,9},{9,8},{10,11... | collective-permute-start | bytes 3145736 | tf_op jit(solution)/shard_map/ppermute | solution.py:110
  263.9 26.2 %collective-permute-start.32 = (bf16[2,256,1024]{2,1,0:T(8,128)(2,1)S(1)}, bf16[2,256,1024]{2,1,0:T(8,128)(2,1)S(1)}, u32[]{:S(2)}, u32[]{:S(2)}) collective-permute-start(bf16[2,256,1024]{2,1,0:T(8,128)(2,1)S(1)} %copy-done.38), channel_id=1, source_target_pairs={{0,1},{1,0},{2,3},{3,2},{4,5},{5,4},{6,7},{7,6},{8,9},{9,8},{10,11... | collective-permute-start | bytes 3145736 | tf_op jit(solution)/shard_map/ppermute | solution.py:110
  266.2 43.3 %collective-permute-start.36 = (bf16[2,256,1024]{2,1,0:T(8,128)(2,1)}, bf16[2,256,1024]{2,1,0:T(8,128)(2,1)S(1)}, u32[]{:S(2)}, u32[]{:S(2)}) collective-permute-start(bf16[2,256,1024]{2,1,0:T(8,128)(2,1)} %get-tuple-element.197), channel_id=1, source_target_pairs={{0,1},{1,0},{2,3},{3,2},{4,5},{5,4},{6,7},{7,6},{8,9},{9,8},{10,11... | collective-permute-start | bytes 3145736 | tf_op jit(solution)/shard_map/ppermute | solution.py:110
  273.5 28.6 %collective-permute-start.35 = (bf16[2,8,128,128]{3,2,1,0:T(8,128)(2,1)}, bf16[2,8,128,128]{3,2,1,0:T(8,128)(2,1)}, u32[]{:S(2)}, u32[]{:S(2)}) collective-permute-start(bf16[2,8,128,128]{3,2,1,0:T(8,128)(2,1)} %get-tuple-element.189), channel_id=1, source_target_pairs={{0,8},{8,0},{16,24},{24,16},{1,9},{9,1},{17,25},{25,17},{2,10},{10... | collective-permute-start | bytes 1572872 | tf_op jit(solution)/shard_map/ppermute | solution.py:154
  275.6 33.8 %collective-permute-start.30 = (bf16[256,1024]{1,0:T(8,128)(2,1)}, bf16[256,1024]{1,0:T(8,128)(2,1)}, u32[]{:S(2)}, u32[]{:S(2)}) collective-permute-start(bf16[256,1024]{1,0:T(8,128)(2,1)} %get-tuple-element.180.refs_1_), channel_id=1, source_target_pairs={{0,2},{1,3},{2,4},{3,5},{4,6},{5,7},{8,10},{9,11},{10,12},{11,13},... | collective-permute-start | bytes 1572872 | tf_op jit(solution)/shard_map/ppermute | solution.py:134
  291.4 58.6 %collective-permute-start.43 = (bf16[2,4,8,128,128]{4,3,2,1,0:T(8,128)(2,1)}, bf16[2,4,8,128,128]{4,3,2,1,0:T(8,128)(2,1)}, u32[]{:S(2)}, u32[]{:S(2)}) collective-permute-start(bf16[2,4,8,128,128]{4,3,2,1,0:T(8,128)(2,1)} %get-tuple-element.215.refs_4_), channel_id=1, source_target_pairs={{0,16},{8,24},{16,0},{24,8},{1,17},{9,25},{17,1},{25,9},{2,18},{10... | collective-permute-start | bytes 6291464 | tf_op jit(solution)/shard_map/ppermute | solution.py:161
  302.1 53.7 %collective-permute-start.44 = (bf16[8,8,128,128]{3,2,1,0:T(8,128)(2,1)}, bf16[8,8,128,128]{3,2,1,0:T(8,128)(2,1)}, u32[]{:S(2)}, u32[]{:S(2)}) collective-permute-start(bf16[8,8,128,128]{3,2,1,0:T(8,128)(2,1)} %get-tuple-element.219), channel_id=1, source_target_pairs={{0,8},{8,0},{16,24},{24,16},{1,9},{9,1},{17,25},{25,17},{2,10},{10... | collective-permute-start | bytes 6291464 | tf_op jit(solution)/shard_map/ppermute | solution.py:154
  309.5 46.4 %collective-permute-start.45 = (bf16[8,8,128,128]{3,2,1,0:T(8,128)(2,1)}, bf16[8,8,128,128]{3,2,1,0:T(8,128)(2,1)}, u32[]{:S(2)}, u32[]{:S(2)}) collective-permute-start(bf16[8,8,128,128]{3,2,1,0:T(8,128)(2,1)} %get-tuple-element.220), channel_id=1, source_target_pairs={{0,8},{8,0},{16,24},{24,16},{1,9},{9,1},{17,25},{25,17},{2,10},{10... | collective-permute-start | bytes 6291464 | tf_op jit(solution)/shard_map/ppermute | solution.py:154
  341.2 24.1 %collective-permute-start.46 = (bf16[2,2,8,128,128]{4,3,2,1,0:T(8,128)(2,1)S(1)}, bf16[2,2,8,128,128]{4,3,2,1,0:T(8,128)(2,1)S(1)}, u32[]{:S(2)}, u32[]{:S(2)}) collective-permute-start(bf16[2,2,8,128,128]{4,3,2,1,0:T(8,128)(2,1)S(1)} %copy-done.24), channel_id=1, source_target_pairs={{0,16},{8,24},{16,0},{24,8},{1,17},{9,25},{17,1},{25,9},{2,18},{10... | collective-permute-start | bytes 3145736 | tf_op jit(solution)/shard_map/ppermute | solution.py:161
  (67 other events, 1219.4 us)

commit v3 on v2

--- a/solution.py
+++ b/solution.py
@@ -15,6 +15,7 @@
 ANY = pl.BlockSpec(memory_space=pl.ANY)
 VMEM_BYTES = 56 * 1024 * 1024
 small_cost = pl.CostEstimate(flops=1000, bytes_accessed=1000, transcendentals=0)
+stagger_cost = pl.CostEstimate(flops=3000000000, bytes_accessed=1000, transcendentals=0)
 
 
 def gelu_pair(value):
@@ -169,14 +170,14 @@
     return parts
 
 
-def load_parts(meta, which, ranges, refs, full, sem):
+def load_parts(meta, ranges, refs, full, sem):
     at, side = meta[0], meta[1]
     for (offset, other, first, last), ref in zip(ranges, refs):
 
         @pl.when((at >= first) & (at <= last))
         def _(offset=offset, other=other, ref=ref):
             slot = (at + offset) * 2 + (1 - side if other else side)
-            pltpu.make_async_copy(ref.at[which], full.at[slot], sem).start()
+            pltpu.make_async_copy(ref, full.at[slot], sem).start()
 
 
 def wait_parts(full, sem):
@@ -204,7 +205,7 @@
 
     @pl.when(row == 0)
     def _():
-        load_parts(meta, 0, ranges, parts, full, sem)
+        load_parts(meta, ranges, parts, full, sem)
         wait_parts(full, sem)
 
     together, blocks, size, _ = w_ref.shape
@@ -219,7 +220,7 @@
 def forward(meta, pat, parts, weights, line):
     rows, blocks, size, _ = weights.shape
     parts, ranges = [p[0] for p in parts], [p[1:] for p in parts]
-    _, tok, width = parts[0].shape
+    tok, width = parts[0].shape
     shards = 2 * line
     together = math.gcd(rows, 8)
     spec = pl.BlockSpec((together, tok, size), lambda r, *_: (r, 0, 0))
@@ -238,7 +239,7 @@
             jax.ShapeDtypeStruct((rows, tok, size), F32),
         ],
         compiler_params=pltpu.CompilerParams(vmem_limit_bytes=VMEM_BYTES),
-        cost_estimate=small_cost,
+        cost_estimate=stagger_cost,
         name="forward_rows",
     )(meta, pat, *parts, weights)
 
@@ -310,7 +311,8 @@
 
 def chunk_kernel(n_after, ranges, spans, start, half, rows, chained, meta, pat, *refs):
     refs = refs[n_after:]
-    parts, refs = refs[: len(ranges)], refs[len(ranges) :]
+    n = len(ranges)
+    x_parts, g_parts, refs = refs[:n], refs[n : 2 * n], refs[2 * n :]
     act_ref, slope_ref, w_ref = refs[:3]
     more, refs = (refs[3 : 3 + 2 * len(spans)], refs[3 + 2 * len(spans) :]) if half == 0 else ((), refs[3:])
     refs = refs[1:] if chained else refs
@@ -321,8 +323,8 @@
 
     @pl.when(step == 0)
     def _():
-        load_parts(meta, 1, ranges, parts, g_full, g_sem)
-        load_parts(meta, 0, ranges, parts, x_full, x_sem)
+        load_parts(meta, ranges, g_parts, g_full, g_sem)
+        load_parts(meta, ranges, x_parts, x_full, x_sem)
         wait_parts(g_full, g_sem)
 
     def store(n, which, i, terms):
@@ -365,10 +367,11 @@
         pl.when(inside)(functools.partial(work, n))
 
 
-def chunk(meta, pat, parts, act, slope, weights, line, start, counts, half, after, more, pg):
+def chunk(meta, pat, x_parts, g_parts, act, slope, weights, line, start, counts, half, after, more, pg):
     rows, blocks, size, _ = weights.shape
-    parts, ranges = [p[0] for p in parts], [p[1:] for p in parts]
-    _, tok, width = parts[0].shape
+    ranges = [p[1:] for p in x_parts]
+    parts = [p[0] for p in x_parts + g_parts]
+    tok, width = parts[0].shape
     spans = [(sum(counts[:n]), count) for n, count in enumerate(counts)]
     together = math.gcd(start, rows // 2, 4, *counts)
 
@@ -482,7 +485,7 @@
 def chunk_counts(half_rows):
     unit = half_rows // 8
     if unit and half_rows == 8 * unit:
-        return [unit, 4 * unit, 2 * unit, unit]
+        return [2 * unit, 3 * unit, 2 * unit, unit]
     return [1] * half_rows
 
 
@@ -500,13 +503,13 @@
     starts = [sum(counts[:n]) for n in range(len(counts))]
     chunks = range(len(counts))
 
-    parts = gather_parts(jnp.stack([tokens, out_grad]), line)
-    act, slope = forward(meta, pat, parts, first_blocks, line)
+    x_parts, g_parts = gather_parts(tokens, line), gather_parts(out_grad, line)
+    act, slope = forward(meta, pat, x_parts, first_blocks, line)
     order = Order(act)
 
     def grad_rows(first, last, half, more, pg):
         run = functools.partial(
-            chunk, meta, pat, parts, act, slope, second_blocks, line, starts[first],
+            chunk, meta, pat, x_parts, g_parts, act, slope, second_blocks, line, starts[first],
             counts[first:last], half,
         )
         return order.kernel(run, more, pg)
@@ -523,8 +526,19 @@
         return [swapped[n : n + 2] for n in range(0, len(swapped), 2)], pg
 
     last = len(counts)
-    sent, pg = other_half(0, last, None)
+    sums = []
+
+    def spread_rows(flip, values, weights):
+        run = functools.partial(spread, flip, meta, pat, line, width)
+        keep, *send = order.kernel(run, values, weights)
+        sums.append(LineSum(keep, send))
+
+    sent, pg = other_half(0, 1, None)
     kept, pg = sum_half(0, 1, pg)
+    if last > 1:
+        more, pg = other_half(1, last, pg)
+        sent += more
+    spread_rows(False, act, second_blocks)
     if last > 1:
         more, pg = sum_half(1, last, pg)
         kept += more
@@ -542,25 +556,23 @@
         return order.kernel(run, own[n], totals)[1]
 
     totals = settle(0, totals)
-    sums = []
-    for flip, values, weights in ((False, act, second_blocks), (True, pg, first_blocks)):
-        run = functools.partial(spread, flip, meta, pat, line, width)
-        keep, *send = order.kernel(run, values, weights)
-        sums.append(LineSum(keep, send))
+    spread_rows(True, pg, first_blocks)
     out, back = sums
     while out.k > 0:
         out.step(order)
     back.step(order)
     for n in range(1, last):
         totals = settle(n, totals)
-        totals = settle_other(n - 1, totals)
-        for item in (out, back, back):
-            if not item.finished():
-                item.step(order)
+        if n < last - 1:
+            for item in (out, back):
+                if not item.finished():
+                    item.step(order)
+            totals = settle_other(n - 1, totals)
+    for n in range(max(last - 2, 0), last):
+        totals = settle_other(n, totals)
     for item in (out, back):
         while not item.finished():
             item.step(order)
-    totals = settle_other(last - 1, totals)
     return (out.total, back.total, totals[1], totals[0])
 
 

time: 380 us -> 358 us (0.942)
  waiting for transfers between devices: 153 us -> 105 us
  starting transfers between devices: 79 us -> 102 us
  Pallas kernels: 125 us -> 131 us
    ppermute x4, waiting for transfers between devices: 35.8 us -> 6.88 us  [__init__(): lax.ppermute(part, 'tensor', swap_pairs(0, self.line - 1))]
    ppermute x4, waiting for transfers between devices: 3.14 us -> 18.3 us  [ring_parts(): lax.ppermute(value, 'dp', [(i, (i + t) % count) for i in range(count)])]
    ppermute x9 -> x18, starting transfers between devices: 16.3 us -> 30.4 us  [gather_parts(): got = lax.ppermute(value, 'tensor', swap_pairs(first, last))]
    ppermute x9 -> x18, waiting for transfers between devices: 18 us -> 5.27 us  [gather_parts(): got = lax.ppermute(value, 'tensor', swap_pairs(first, last))]
    ppermute x3 -> x6, waiting for transfers between devices: 19.5 us -> 7.59 us  [gather_parts(): up = lax.ppermute(from_up, 'tensor', line_pairs(line, 1, k, line - 2))]
    ppermute x3 -> x6, waiting for transfers between devices: 45.6 us -> 36.4 us  [gather_parts(): lax.ppermute(from_down, 'tensor', line_pairs(line, -1, 1, line - 1 - k))]
    ppermute x3 -> x6, starting transfers between devices: 7.64 us -> 13.8 us  [gather_parts(): up = lax.ppermute(from_up, 'tensor', line_pairs(line, 1, k, line - 2))]
    pallas_call x3 -> x4, Pallas kernels: 43.9 us -> 49.7 us  [chunk(): pl.pallas_call(functools.partial(chunk_kernel, len(after), ranges, spans,...]
  transfers between devices with their start and end apart: 51 -> 66, of which waited for: 17 -> 21; matrix products, arithmetic and copies ran while one was open for 3% -> 3% of each run, Pallas kernels for 24% -> 31%
where the time goes in v3:
time: 358 us; the launch traced here: 356 us
  Pallas kernels  131 us (37%)
  waiting for transfers between devices  105 us (29%)
  starting transfers between devices  102 us (28%)
  other arithmetic  10.1 us (3%)
  local copies, waits for them, and re-layouts  6.88 us (2%)
    pallas_call x4, Pallas kernels, chunk(): pl.pallas_call(functools.partial(chunk_kernel, len(after), ranges, spans,...  49.7 us
    ppermute x6, waiting for transfers between devices, gather_parts(): lax.ppermute(from_down, 'tensor', line_pairs(line, -1, 1, line - 1 - k))  36.4 us
    pallas_call x8, Pallas kernels, place(): pl.pallas_call(functools.partial(place_kernel, len(after), n, into is not...  34.5 us
    ppermute x6, starting transfers between devices, step(): lax.ppermute(up, 'tensor', line_pairs(line, 1, 0, line - 1 - k))  32.7 us
    pallas_call x2, Pallas kernels, spread(): pl.pallas_call(functools.partial(spread_kernel, flip, len(after), line),...  32.6 us
    ppermute x18, starting transfers between devices, gather_parts(): got = lax.ppermute(value, 'tensor', swap_pairs(first, last))  30.4 us
    ppermute x6, waiting for transfers between devices, step(): lax.ppermute(up, 'tensor', line_pairs(line, 1, 0, line - 1 - k))  18.9 us
    ppermute x4, waiting for transfers between devices, ring_parts(): lax.ppermute(value, 'dp', [(i, (i + t) % count) for i in range(count)])  18.3 us
  transfers between devices with their start and end apart: 66, of which 21 were waited for; matrix products, arithmetic and copies ran while one was open for 3% of the time, Pallas kernels for 31%

profile of v3, /device:TPU:0, one launch (start us, length us, event | category | flops | bytes accessed | tf_op | source)
XLA Modules:
  0.0 356.3 jit_solution(12001083105537181069)
XLA Ops:
  0.6 5.0 %collective-permute-start = (bf16[256,1024]{1,0:T(8,128)(2,1)}, bf16[256,1024]{1,0:T(8,128)(2,1)S(1)}, u32[]{:S(2)}, u32[]{:S(2)}) collective-permute-start(bf16[256,1024]{1,0:T(8,128)(2,1)} %refs_1_.7), channel_id=1, source_target_pairs={{0,2},{1,3},{2,4},{3,5},{4,6},{5,7},{8,10},{9,11},{10,12},{11,13},... | collective-permute-start | bytes 1572872 | tf_op jit(solution)/shard_map/ppermute | solution.py:60
  8.5 4.6 %collective-permute-start.15 = (bf16[256,1024]{1,0:T(8,128)(2,1)}, bf16[256,1024]{1,0:T(8,128)(2,1)S(1)}, u32[]{:S(2)}, u32[]{:S(2)}) collective-permute-start(bf16[256,1024]{1,0:T(8,128)(2,1)} %refs_17_.7), channel_id=1, source_target_pairs={{0,2},{1,3},{2,4},{3,5},{4,6},{5,7},{8,10},{9,11},{10,12},{11,13},... | collective-permute-start | bytes 1572872 | tf_op jit(solution)/shard_map/ppermute | solution.py:60
  35.9 7.6 %collective-permute-done.4.refs_5_.refs_6_ = bf16[256,1024]{1,0:T(8,128)(2,1)S(1)} collective-permute-done((bf16[256,1024]{1,0:T(8,128)(2,1)S(1)}, bf16[256,1024]{1,0:T(8,128)(2,1)S(1)}, u32[]{:S(2)}, u32[]{:S(2)}) %collective-permute-start.4) | collective-permute-done | bytes 524320 | tf_op jit(solution)/shard_map/ppermute | solution.py:61
  52.7 8.6 %collective-permute-done.19.refs_22_ = bf16[256,1024]{1,0:T(8,128)(2,1)S(1)} collective-permute-done((bf16[256,1024]{1,0:T(8,128)(2,1)S(1)}, bf16[256,1024]{1,0:T(8,128)(2,1)S(1)}, u32[]{:S(2)}, u32[]{:S(2)}) %collective-permute-start.19) | collective-permute-done | bytes 524320 | tf_op jit(solution)/shard_map/ppermute | solution.py:61
  67.9 7.0 %collective-permute-done.8.refs_9_.refs_10_ = bf16[256,1024]{1,0:T(8,128)(2,1)} collective-permute-done((bf16[256,1024]{1,0:T(8,128)(2,1)S(1)}, bf16[256,1024]{1,0:T(8,128)(2,1)}, u32[]{:S(2)}, u32[]{:S(2)}) %collective-permute-start.8) | collective-permute-done | bytes 524320 | tf_op jit(solution)/shard_map/ppermute | solution.py:61
  84.4 8.2 %collective-permute-done.23.refs_26_ = bf16[256,1024]{1,0:T(8,128)(2,1)} collective-permute-done((bf16[256,1024]{1,0:T(8,128)(2,1)S(1)}, bf16[256,1024]{1,0:T(8,128)(2,1)}, u32[]{:S(2)}, u32[]{:S(2)}) %collective-permute-start.23) | collective-permute-done | bytes 524320 | tf_op jit(solution)/shard_map/ppermute | solution.py:61
  99.5 4.8 %collective-permute-done.13.refs_14_.refs_15_ = bf16[256,1024]{1,0:T(8,128)(2,1)} collective-permute-done((bf16[256,1024]{1,0:T(8,128)(2,1)}, bf16[256,1024]{1,0:T(8,128)(2,1)}, u32[]{:S(2)}, u32[]{:S(2)}) %collective-permute-start.13) | collective-permute-done | bytes 524320 | tf_op jit(solution)/shard_map/ppermute | solution.py:75
  104.4 14.1 %forward_rows.1 = (bf16[32,256,128]{2,1,0:T(8,128)(2,1)}, f32[32,256,128]{2,1,0:T(8,128)}) custom-call(s32[3]{0:T(128)} %pad_add_fusion.meta, s32[256]{0:T(256)} %reshape.55.pat, bf16[256,1024]{1,0:T(8,128)(2,1)} %refs_1_.7, bf16[256,1024]{1,0:T(8,128)(2,1)} %copy-done, bf16[256,1024]{1,0:T(8,128)(2,1)} %copy-done.1, bf16[256,1024]{1,0:T(8,128)(2,1)} %copy-done.2, ...), custom_call_target="tpu_custom_call" | custom-call | flops 3000000000 | bytes 1000 | tf_op jit(solution)/shard_map/forward_rows/pallas_call | solution.py:227
  118.6 8.7 %grad_rows.4 = (bf16[4,8,128,128]{3,2,1,0:T(8,128)(2,1)}, bf16[4,8,128,128]{3,2,1,0:T(8,128)(2,1)}, bf16[32,256,128]{2,1,0:T(8,128)(2,1)}) custom-call(s32[3]{0:T(128)} %pad_add_fusion.meta, s32[256]{0:T(256)} %reshape.55.pat, bf16[32,256,128]{2,1,0:T(8,128)(2,1)} %get-tuple-element.148.refs_0_.refs_33_.refs_1_, bf16[256,1024]{1,0:T(8,128)(2,1)} %refs_1_.7, ...), custom_call_target="tpu_custom_call" | custom-call | flops 1000 | bytes 1000 | tf_op jit(solution)/shard_map/grad_rows/pallas_call | solution.py:408
  132.7 9.5 %grad_rows.5 = (bf16[2,4,8,128,128]{4,3,2,1,0:T(8,128)(2,1)}, bf16[32,256,128]{2,1,0:T(8,128)(2,1)}) custom-call(s32[3]{0:T(128)} %pad_add_fusion.meta, s32[256]{0:T(256)} %reshape.55.pat, bf16[4,8,128,128]{3,2,1,0:T(8,128)(2,1)} %get-tuple-element.163.refs_0_, bf16[256,1024]{1,0:T(8,128)(2,1)} %refs_1_.7, ...), custom_call_target="tpu_custom_call", output_to_operand_aliasing={{1}: (40, {})} | custom-call | flops 1000 | bytes 1000 | tf_op jit(solution)/shard_map/grad_rows/pallas_call | solution.py:408
  143.8 15.0 %grad_rows.6 = (bf16[6,8,128,128]{3,2,1,0:T(8,128)(2,1)}, bf16[6,8,128,128]{3,2,1,0:T(8,128)(2,1)}, bf16[4,8,128,128]{3,2,1,0:T(8,128)(2,1)}, bf16[4,8,128,128]{...) custom-call(s32[3]{0:T(128)} %pad_add_fusion.meta, ...), custom_call_target="tpu_custom_call", output_to_operand_aliasing={{6}: (38, {})} | custom-call | flops 1000 | bytes 1000 | tf_op jit(solution)/shard_map/grad_rows/pallas_call | solution.py:408
  161.9 16.1 %spread_out.1 = (bf16[4,256,1024]{2,1,0:T(8,128)(2,1)}, bf16[2,256,1024]{2,1,0:T(8,128)(2,1)}, bf16[2,256,1024]{2,1,0:T(8,128)(2,1)}) custom-call(s32[3]{0:T(128)} %pad_add_fusion.meta, s32[256]{0:T(256)} %reshape.55.pat, bf16[6,8,128,128]{3,2,1,0:T(8,128)(2,1)} %get-tuple-element.168.refs_0_, ...), custom_call_target="tpu_custom_call" | custom-call | flops 1000 | bytes 1000 | tf_op jit(solution)/shard_map/spread_out/pallas_call | solution.py:287
  180.3 16.5 %grad_rows.7 = (bf16[2,6,8,128,128]{4,3,2,1,0:T(8,128)(2,1)}, bf16[2,4,8,128,128]{4,3,2,1,0:T(8,128)(2,1)}, bf16[2,2,8,128,128]{4,3,2,1,0:T(8,128)(2,1)}, bf16[32,256,128]{2,1,0:T(8,128)(2,1)}) custom-call(s32[3]{0:T(128)} %pad_add_fusion.meta, s32[256]{0:T(256)} %reshape.55.pat, ...), custom_call_target="tpu_custom_call", output_to_operand_aliasing={{3}: (44, {})} | custom-call | flops 1000 | bytes 1000 | tf_op jit(solution)/shard_map/grad_rows/pallas_call | solution.py:408
  203.3 16.5 %spread_back.1 = (bf16[4,256,1024]{2,1,0:T(8,128)(2,1)}, bf16[2,256,1024]{2,1,0:T(8,128)(2,1)}, bf16[2,256,1024]{2,1,0:T(8,128)(2,1)}) custom-call(s32[3]{0:T(128)} %pad_add_fusion.meta, s32[256]{0:T(256)} %reshape.55.pat, s32[8,128]{1,0:T(8,128)} %get-tuple-element.180.refs_0_, bf16[32,256,128]{2,1,0:T(8,128)(2,1)} %get-tuple-element.181.refs_1_, ...), custom_call_target="tpu_custom_call" | custom-call | flops 1000 | bytes 1000 | tf_op jit(solution)/shard_map/spread_back/pallas_call | solution.py:287
  220.3 4.6 %collective-permute-start.41 = (bf16[256,1024]{1,0:T(8,128)(2,1)S(1)}, bf16[256,1024]{1,0:T(8,128)(2,1)S(1)}, u32[]{:S(2)}, u32[]{:S(2)}) collective-permute-start(bf16[256,1024]{1,0:T(8,128)(2,1)S(1)} %get-tuple-element.207.refs_3_), channel_id=1, source_target_pairs={{0,2},{1,3},{8,10},{9,11},{16,18},{17,19},{24,26},{25,27}} | collective-permute-start | bytes 1572872 | tf_op jit(solution)/shard_map/ppermute | solution.py:135
  227.0 9.3 %collective-permute-done.41 = bf16[256,1024]{1,0:T(8,128)(2,1)S(1)} collective-permute-done((bf16[256,1024]{1,0:T(8,128)(2,1)S(1)}, bf16[256,1024]{1,0:T(8,128)(2,1)S(1)}, u32[]{:S(2)}, u32[]{:S(2)}) %collective-permute-start.41) | collective-permute-done | bytes 524320 | tf_op jit(solution)/shard_map/ppermute | solution.py:135
  242.7 9.1 %collective-permute-done.43 = bf16[256,1024]{1,0:T(8,128)(2,1)S(1)} collective-permute-done((bf16[256,1024]{1,0:T(8,128)(2,1)S(1)}, bf16[256,1024]{1,0:T(8,128)(2,1)S(1)}, u32[]{:S(2)}, u32[]{:S(2)}) %collective-permute-start.43) | collective-permute-done | bytes 524320 | tf_op jit(solution)/shard_map/ppermute | solution.py:135
  252.6 11.0 %collective-permute-start.45 = (bf16[256,1024]{1,0:T(8,128)(2,1)S(1)}, bf16[256,1024]{1,0:T(8,128)(2,1)S(1)}, u32[]{:S(2)}, u32[]{:S(2)}) collective-permute-start(bf16[256,1024]{1,0:T(8,128)(2,1)S(1)} %get-tuple-element.205.refs_1_), channel_id=1, source_target_pairs={{0,2},{1,3},{2,4},{3,5},{4,6},{5,7},{8,10},{9,11},{10,12},{11,13},... | collective-permute-start | bytes 1572872 | tf_op jit(solution)/shard_map/ppermute | solution.py:135
  266.1 6.9 %collective-permute-done.49 = bf16[2,256,1024]{2,1,0:T(8,128)(2,1)S(1)} collective-permute-done((bf16[2,256,1024]{2,1,0:T(8,128)(2,1)S(1)}, bf16[2,256,1024]{2,1,0:T(8,128)(2,1)S(1)}, u32[]{:S(2)}, u32[]{:S(2)}) %collective-permute-start.49) | collective-permute-done | bytes 1048608 | tf_op jit(solution)/shard_map/ppermute | solution.py:111
  278.3 7.5 %place_rows.9 = (s32[8,128]{1,0:T(8,128)}, bf16[32,8,128,128]{3,2,1,0:T(8,128)(2,1)}, bf16[32,8,128,128]{3,2,1,0:T(8,128)(2,1)}, bf16[6,8,128,128]{3,2,1,0:T(8,128)(2,1)}, bf16[6,8,128,128]{3,2,1,0:T(8,128)(2,1)}) custom-call(s32[3]{0:T(128)} %pad_add_fusion.meta, bf16[256,1024]{1,0:T(8,128)(2,1)} %copy-done.27, ...), custom_call_target="tpu_custom_call", output_to_operand_aliasing={{1}: (8, {}), {2}: (9, {})} | custom-call | flops 1000 | bytes 1000 | tf_op jit(solution)/shard_map/place_rows/pallas_call | solution.py:468
  296.1 16.2 %collective-permute-done.56.refs_2_ = bf16[2,4,8,128,128]{4,3,2,1,0:T(8,128)(2,1)} collective-permute-done((bf16[2,4,8,128,128]{4,3,2,1,0:T(8,128)(2,1)}, bf16[2,4,8,128,128]{4,3,2,1,0:T(8,128)(2,1)}, u32[]{:S(2)}, u32[]{:S(2)}) %collective-permute-start.56) | collective-permute-done | bytes 2097184 | tf_op jit(solution)/shard_map/ppermute | solution.py:162
  323.2 5.2 %collective-permute-start.57 = (bf16[256,1024]{1,0:T(8,128)(2,1)S(1)}, bf16[256,1024]{1,0:T(8,128)(2,1)S(1)}, u32[]{:S(2)}, u32[]{:S(2)}) collective-permute-start(bf16[256,1024]{1,0:T(8,128)(2,1)S(1)} %get-tuple-element.267.refs_0_), channel_id=1, source_target_pairs={{0,2},{1,3},{2,4},{3,5},{4,6},{5,7},{8,10},{9,11},{10,12},{11,13},... | collective-permute-start | bytes 1572872 | tf_op jit(solution)/shard_map/ppermute | solution.py:135
  329.7 5.0 %place_rows.12 = (s32[8,128]{1,0:T(8,128)}, bf16[32,8,128,128]{3,2,1,0:T(8,128)(2,1)}, bf16[32,8,128,128]{3,2,1,0:T(8,128)(2,1)}) custom-call(s32[3]{0:T(128)} %pad_add_fusion.meta, bf16[256,1024]{1,0:T(8,128)(2,1)} %copy-done.30, s32[8,128]{1,0:T(8,128)} %get-tuple-element.245.refs_1_, ...), custom_call_target="tpu_custom_call", output_to_operand_aliasing={{1}: (5, {}), {2}: (6, {})} | custom-call | flops 1000 | bytes 1000 | tf_op jit(solution)/shard_map/place_rows/pallas_call | solution.py:468
  340.9 6.0 %collective-permute-done.58 = bf16[256,1024]{1,0:T(8,128)(2,1)S(1)} collective-permute-done((bf16[256,1024]{1,0:T(8,128)(2,1)S(1)}, bf16[256,1024]{1,0:T(8,128)(2,1)S(1)}, u32[]{:S(2)}, u32[]{:S(2)}) %collective-permute-start.58) | collective-permute-done | bytes 524320 | tf_op jit(solution)/shard_map/ppermute | solution.py:136
  (228 shorter events, 131.6 us)
Async XLA Ops:
  8.5 19.8 %collective-permute-start.15 = (bf16[256,1024]{1,0:T(8,128)(2,1)}, bf16[256,1024]{1,0:T(8,128)(2,1)S(1)}, u32[]{:S(2)}, u32[]{:S(2)}) collective-permute-start(bf16[256,1024]{1,0:T(8,128)(2,1)} %refs_17_.7), channel_id=1, source_target_pairs={{0,2},{1,3},{2,4},{3,5},{4,6},{5,7},{8,10},{9,11},{10,12},{11,13},... | collective-permute-start | bytes 1572872 | tf_op jit(solution)/shard_map/ppermute | solution.py:60
  13.0 20.8 %collective-permute-start.16 = (bf16[256,1024]{1,0:T(8,128)(2,1)}, bf16[256,1024]{1,0:T(8,128)(2,1)S(1)}, u32[]{:S(2)}, u32[]{:S(2)}) collective-permute-start(bf16[256,1024]{1,0:T(8,128)(2,1)} %refs_17_.7), channel_id=1, source_target_pairs={{2,0},{3,1},{4,2},{5,3},{6,4},{7,5},{10,8},{11,9},{12,10},{13,11},... | collective-permute-start | bytes 1572872 | tf_op jit(solution)/shard_map/ppermute | solution.py:61
  23.3 20.3 %collective-permute-start.4 = (bf16[256,1024]{1,0:T(8,128)(2,1)S(1)}, bf16[256,1024]{1,0:T(8,128)(2,1)S(1)}, u32[]{:S(2)}, u32[]{:S(2)}) collective-permute-start(bf16[256,1024]{1,0:T(8,128)(2,1)S(1)} %collective-permute-done.1.refs_2_.refs_3_), channel_id=1, source_target_pairs={{2,0},{3,1},{4,2},{5,3},{10,8},{11,9},{12,10},{13,11},{18,16},{19,... | collective-permute-start | bytes 1572872 | tf_op jit(solution)/shard_map/ppermute | solution.py:61
  79.5 24.9 %collective-permute-start.13 = (bf16[256,1024]{1,0:T(8,128)(2,1)}, bf16[256,1024]{1,0:T(8,128)(2,1)}, u32[]{:S(2)}, u32[]{:S(2)}) collective-permute-start(bf16[256,1024]{1,0:T(8,128)(2,1)} %collective-permute-done.8.refs_9_.refs_10_), channel_id=1, source_target_pairs={{0,1},{1,0},{8,9},{9,8},{16,17},{17,16},{24,25},{25,24}} | collective-permute-start | bytes 1572872 | tf_op jit(solution)/shard_map/ppermute | solution.py:75
  82.9 21.4 %collective-permute-start.14 = (bf16[256,1024]{1,0:T(8,128)(2,1)}, bf16[256,1024]{1,0:T(8,128)(2,1)}, u32[]{:S(2)}, u32[]{:S(2)}) collective-permute-start(bf16[256,1024]{1,0:T(8,128)(2,1)} %collective-permute-done.7.refs_8_.refs_9_), channel_id=1, source_target_pairs={{6,7},{7,6},{14,15},{15,14},{22,23},{23,22},{30,31},{31,30}} | collective-permute-start | bytes 1572872 | tf_op jit(solution)/shard_map/ppermute | solution.py:75
  93.0 25.5 %collective-permute-start.28 = (bf16[256,1024]{1,0:T(8,128)(2,1)}, bf16[256,1024]{1,0:T(8,128)(2,1)}, u32[]{:S(2)}, u32[]{:S(2)}) collective-permute-start(bf16[256,1024]{1,0:T(8,128)(2,1)} %collective-permute-done.23.refs_26_), channel_id=1, source_target_pairs={{0,1},{1,0},{8,9},{9,8},{16,17},{17,16},{24,25},{25,24}} | collective-permute-start | bytes 1572872 | tf_op jit(solution)/shard_map/ppermute | solution.py:75
  96.0 22.5 %collective-permute-start.29 = (bf16[256,1024]{1,0:T(8,128)(2,1)}, bf16[256,1024]{1,0:T(8,128)(2,1)}, u32[]{:S(2)}, u32[]{:S(2)}) collective-permute-start(bf16[256,1024]{1,0:T(8,128)(2,1)} %collective-permute-done.22.refs_25_), channel_id=1, source_target_pairs={{6,7},{7,6},{14,15},{15,14},{22,23},{23,22},{30,31},{31,30}} | collective-permute-start | bytes 1572872 | tf_op jit(solution)/shard_map/ppermute | solution.py:75
  142.2 54.7 %collective-permute-start.40 = (bf16[2,4,8,128,128]{4,3,2,1,0:T(8,128)(2,1)}, bf16[2,4,8,128,128]{4,3,2,1,0:T(8,128)(2,1)S(1)}, u32[]{:S(2)}, u32[]{:S(2)}) collective-permute-start(bf16[2,4,8,128,128]{4,3,2,1,0:T(8,128)(2,1)} %get-tuple-element.166.refs_0_.refs_1_), channel_id=1, source_target_pairs={{0,16},{8,24},{16,0},{24,8},{1,17},{9,25},{17,1},{25,9},{2,18},{10... | collective-permute-start | bytes 6291464 | tf_op jit(solution)/shard_map/ppermute | solution.py:162
  159.4 19.2 %collective-permute-start.34 = (bf16[6,8,128,128]{3,2,1,0:T(8,128)(2,1)}, bf16[6,8,128,128]{3,2,1,0:T(8,128)(2,1)S(1)}, u32[]{:S(2)}, u32[]{:S(2)}) collective-permute-start(bf16[6,8,128,128]{3,2,1,0:T(8,128)(2,1)} %get-tuple-element.168.refs_0_), channel_id=1, source_target_pairs={{0,8},{8,0},{16,24},{24,16},{1,9},{9,1},{17,25},{25,17},{2,10},{10... | collective-permute-start | bytes 4718600 | tf_op jit(solution)/shard_map/ppermute | solution.py:155
  159.5 19.1 %collective-permute-start.35 = (bf16[6,8,128,128]{3,2,1,0:T(8,128)(2,1)}, bf16[6,8,128,128]{3,2,1,0:T(8,128)(2,1)S(1)}, u32[]{:S(2)}, u32[]{:S(2)}) collective-permute-start(bf16[6,8,128,128]{3,2,1,0:T(8,128)(2,1)} %get-tuple-element.172), channel_id=1, source_target_pairs={{0,8},{8,0},{16,24},{24,16},{1,9},{9,1},{17,25},{25,17},{2,10},{10... | collective-permute-start | bytes 4718600 | tf_op jit(solution)/shard_map/ppermute | solution.py:155
  178.0 41.9 %collective-permute-start.33 = (bf16[2,256,1024]{2,1,0:T(8,128)(2,1)}, bf16[2,256,1024]{2,1,0:T(8,128)(2,1)S(1)}, u32[]{:S(2)}, u32[]{:S(2)}) collective-permute-start(bf16[2,256,1024]{2,1,0:T(8,128)(2,1)} %get-tuple-element.171), channel_id=1, source_target_pairs={{0,1},{1,0},{2,3},{3,2},{4,5},{5,4},{6,7},{7,6},{8,9},{9,8},{10,11... | collective-permute-start | bytes 3145736 | tf_op jit(solution)/shard_map/ppermute | solution.py:111
  196.9 80.7 %collective-permute-start.48 = (bf16[2,6,8,128,128]{4,3,2,1,0:T(8,128)(2,1)}, bf16[2,6,8,128,128]{4,3,2,1,0:T(8,128)(2,1)}, u32[]{:S(2)}, u32[]{:S(2)}) collective-permute-start(bf16[2,6,8,128,128]{4,3,2,1,0:T(8,128)(2,1)} %get-tuple-element.209.refs_0_.refs_5_), channel_id=1, source_target_pairs={{0,16},{8,24},{16,0},{24,8},{1,17},{9,25},{17,1},{25,9},{2,18},{10... | collective-permute-start | bytes 9437192 | tf_op jit(solution)/shard_map/ppermute | solution.py:162
  197.4 29.5 %collective-permute-start.32 = (bf16[2,256,1024]{2,1,0:T(8,128)(2,1)}, bf16[2,256,1024]{2,1,0:T(8,128)(2,1)S(1)}, u32[]{:S(2)}, u32[]{:S(2)}) collective-permute-start(bf16[2,256,1024]{2,1,0:T(8,128)(2,1)} %get-tuple-element.170), channel_id=1, source_target_pairs={{0,1},{1,0},{2,3},{3,2},{4,5},{5,4},{6,7},{7,6},{8,9},{9,8},{10,11... | collective-permute-start | bytes 3145736 | tf_op jit(solution)/shard_map/ppermute | solution.py:111
  225.6 38.0 %collective-permute-start.47 = (bf16[2,256,1024]{2,1,0:T(8,128)(2,1)S(1)}, bf16[2,256,1024]{2,1,0:T(8,128)(2,1)S(1)}, u32[]{:S(2)}, u32[]{:S(2)}) collective-permute-start(bf16[2,256,1024]{2,1,0:T(8,128)(2,1)S(1)} %copy-done.46), channel_id=1, source_target_pairs={{0,1},{1,0},{2,3},{3,2},{4,5},{5,4},{6,7},{7,6},{8,9},{9,8},{10,11... | collective-permute-start | bytes 3145736 | tf_op jit(solution)/shard_map/ppermute | solution.py:111
  241.9 31.2 %collective-permute-start.49 = (bf16[2,256,1024]{2,1,0:T(8,128)(2,1)S(1)}, bf16[2,256,1024]{2,1,0:T(8,128)(2,1)S(1)}, u32[]{:S(2)}, u32[]{:S(2)}) collective-permute-start(bf16[2,256,1024]{2,1,0:T(8,128)(2,1)S(1)} %copy-done.45), channel_id=1, source_target_pairs={{0,1},{1,0},{2,3},{3,2},{4,5},{5,4},{6,7},{7,6},{8,9},{9,8},{10,11... | collective-permute-start | bytes 3145736 | tf_op jit(solution)/shard_map/ppermute | solution.py:111
  251.8 60.5 %collective-permute-start.56 = (bf16[2,4,8,128,128]{4,3,2,1,0:T(8,128)(2,1)}, bf16[2,4,8,128,128]{4,3,2,1,0:T(8,128)(2,1)}, u32[]{:S(2)}, u32[]{:S(2)}) collective-permute-start(bf16[2,4,8,128,128]{4,3,2,1,0:T(8,128)(2,1)} %get-tuple-element.232.refs_1_), channel_id=1, source_target_pairs={{0,16},{8,24},{16,0},{24,8},{1,17},{9,25},{17,1},{25,9},{2,18},{10... | collective-permute-start | bytes 6291464 | tf_op jit(solution)/shard_map/ppermute | solution.py:162
  252.6 23.4 %collective-permute-start.45 = (bf16[256,1024]{1,0:T(8,128)(2,1)S(1)}, bf16[256,1024]{1,0:T(8,128)(2,1)S(1)}, u32[]{:S(2)}, u32[]{:S(2)}) collective-permute-start(bf16[256,1024]{1,0:T(8,128)(2,1)S(1)} %get-tuple-element.205.refs_1_), channel_id=1, source_target_pairs={{0,2},{1,3},{2,4},{3,5},{4,6},{5,7},{8,10},{9,11},{10,12},{11,13},... | collective-permute-start | bytes 1572872 | tf_op jit(solution)/shard_map/ppermute | solution.py:135
  286.2 36.9 %collective-permute-start.59 = (bf16[6,8,128,128]{3,2,1,0:T(8,128)(2,1)}, bf16[6,8,128,128]{3,2,1,0:T(8,128)(2,1)}, u32[]{:S(2)}, u32[]{:S(2)}) collective-permute-start(bf16[6,8,128,128]{3,2,1,0:T(8,128)(2,1)} %get-tuple-element.246), channel_id=1, source_target_pairs={{0,8},{8,0},{16,24},{24,16},{1,9},{9,1},{17,25},{25,17},{2,10},{10... | collective-permute-start | bytes 4718600 | tf_op jit(solution)/shard_map/ppermute | solution.py:155
  286.2 42.1 %collective-permute-start.60 = (bf16[6,8,128,128]{3,2,1,0:T(8,128)(2,1)}, bf16[6,8,128,128]{3,2,1,0:T(8,128)(2,1)}, u32[]{:S(2)}, u32[]{:S(2)}) collective-permute-start(bf16[6,8,128,128]{3,2,1,0:T(8,128)(2,1)} %get-tuple-element.247), channel_id=1, source_target_pairs={{0,8},{8,0},{16,24},{24,16},{1,9},{9,1},{17,25},{25,17},{2,10},{10... | collective-permute-start | bytes 4718600 | tf_op jit(solution)/shard_map/ppermute | solution.py:155
  290.8 29.7 %collective-permute-start.52 = (bf16[256,1024]{1,0:T(8,128)(2,1)S(1)}, bf16[256,1024]{1,0:T(8,128)(2,1)S(1)}, u32[]{:S(2)}, u32[]{:S(2)}) collective-permute-start(bf16[256,1024]{1,0:T(8,128)(2,1)S(1)} %get-tuple-element.269.refs_0_), channel_id=1, source_target_pairs={{0,2},{1,3},{2,4},{3,5},{8,10},{9,11},{10,12},{11,13},{16,18},{17,... | collective-permute-start | bytes 1572872 | tf_op jit(solution)/shard_map/ppermute | solution.py:135
  295.4 25.3 %collective-permute-start.53 = (bf16[256,1024]{1,0:T(8,128)(2,1)S(1)}, bf16[256,1024]{1,0:T(8,128)(2,1)S(1)}, u32[]{:S(2)}, u32[]{:S(2)}) collective-permute-start(bf16[256,1024]{1,0:T(8,128)(2,1)S(1)} %get-tuple-element.268), channel_id=1, source_target_pairs={{4,2},{5,3},{6,4},{7,5},{12,10},{13,11},{14,12},{15,13},{20,18},{2... | collective-permute-start | bytes 1572872 | tf_op jit(solution)/shard_map/ppermute | solution.py:136
  312.3 24.4 %collective-permute-start.61 = (bf16[2,2,8,128,128]{4,3,2,1,0:T(8,128)(2,1)S(1)}, bf16[2,2,8,128,128]{4,3,2,1,0:T(8,128)(2,1)}, u32[]{:S(2)}, u32[]{:S(2)}) collective-permute-start(bf16[2,2,8,128,128]{4,3,2,1,0:T(8,128)(2,1)S(1)} %copy-done.33), channel_id=1, source_target_pairs={{0,16},{8,24},{16,0},{24,8},{1,17},{9,25},{17,1},{25,9},{2,18},{10... | collective-permute-start | bytes 3145736 | tf_op jit(solution)/shard_map/ppermute | solution.py:162
  320.6 27.5 %collective-permute-start.62 = (bf16[4,8,128,128]{3,2,1,0:T(8,128)(2,1)}, bf16[4,8,128,128]{3,2,1,0:T(8,128)(2,1)S(1)}, u32[]{:S(2)}, u32[]{:S(2)}) collective-permute-start(bf16[4,8,128,128]{3,2,1,0:T(8,128)(2,1)} %get-tuple-element.255), channel_id=1, source_target_pairs={{0,8},{8,0},{16,24},{24,16},{1,9},{9,1},{17,25},{25,17},{2,10},{10... | collective-permute-start | bytes 3145736 | tf_op jit(solution)/shard_map/ppermute | solution.py:155
  320.7 27.4 %collective-permute-start.63 = (bf16[4,8,128,128]{3,2,1,0:T(8,128)(2,1)}, bf16[4,8,128,128]{3,2,1,0:T(8,128)(2,1)}, u32[]{:S(2)}, u32[]{:S(2)}) collective-permute-start(bf16[4,8,128,128]{3,2,1,0:T(8,128)(2,1)} %get-tuple-element.256), channel_id=1, source_target_pairs={{0,8},{8,0},{16,24},{24,16},{1,9},{9,1},{17,25},{25,17},{2,10},{10... | collective-permute-start | bytes 3145736 | tf_op jit(solution)/shard_map/ppermute | solution.py:155
  (89 other events, 1639.1 us)

commit v4 on v3

--- a/solution.py
+++ b/solution.py
@@ -485,7 +485,7 @@
 def chunk_counts(half_rows):
     unit = half_rows // 8
     if unit and half_rows == 8 * unit:
-        return [2 * unit, 3 * unit, 2 * unit, unit]
+        return [2 * unit, 3 * unit, 3 * unit]
     return [1] * half_rows
 
 
@@ -563,13 +563,15 @@
     back.step(order)
     for n in range(1, last):
         totals = settle(n, totals)
-        if n < last - 1:
-            for item in (out, back):
-                if not item.finished():
-                    item.step(order)
+        if n == 1:
+            out.step(order)
+            back.step(order)
+            totals = settle_other(0, totals)
+            while not back.finished():
+                back.step(order)
+        if n > 1 or last == 2:
             totals = settle_other(n - 1, totals)
-    for n in range(max(last - 2, 0), last):
-        totals = settle_other(n, totals)
+    totals = settle_other(last - 1, totals)
     for item in (out, back):
         while not item.finished():
             item.step(order)

time: 358 us -> 358 us (level)
  starting transfers between devices: 102 us -> 110 us
  waiting for transfers between devices: 105 us -> 98.2 us
    ppermute x4 -> x3, waiting for transfers between devices: 18.3 us -> 0.01 us  [ring_parts(): lax.ppermute(value, 'dp', [(i, (i + t) % count) for i in range(count)])]
    ppermute x6, waiting for transfers between devices: 18.9 us -> 36.4 us  [step(): lax.ppermute(up, 'tensor', line_pairs(line, 1, 0, line - 1 - k))]
    ppermute x6, starting transfers between devices: 32.7 us -> 41.8 us  [step(): lax.ppermute(up, 'tensor', line_pairs(line, 1, 0, line - 1 - k))]
    pallas_call x8 -> x6, Pallas kernels: 34.5 us -> 32.1 us  [place(): pl.pallas_call(functools.partial(place_kernel, len(after), n, into is not...]
  transfers between devices with their start and end apart: 66 -> 61, of which waited for: 21 -> 20; matrix products, arithmetic and copies ran while one was open for 3% -> 3% of each run, Pallas kernels for 31% -> 30%
where the time goes in v4:
time: 358 us; the launch traced here: 354 us
  Pallas kernels  128 us (36%)
  starting transfers between devices  110 us (31%)
  waiting for transfers between devices  98.2 us (27%)
  other arithmetic  9.8 us (3%)
  local copies, waits for them, and re-layouts  7.03 us (2%)
    pallas_call x4, Pallas kernels, chunk(): pl.pallas_call(functools.partial(chunk_kernel, len(after), ranges, spans,...  49.4 us
    ppermute x6, starting transfers between devices, step(): lax.ppermute(up, 'tensor', line_pairs(line, 1, 0, line - 1 - k))  41.8 us
    ppermute x6, waiting for transfers between devices, step(): lax.ppermute(up, 'tensor', line_pairs(line, 1, 0, line - 1 - k))  36.4 us
    ppermute x6, waiting for transfers between devices, gather_parts(): lax.ppermute(from_down, 'tensor', line_pairs(line, -1, 1, line - 1 - k))  36.3 us
    pallas_call x2, Pallas kernels, spread(): pl.pallas_call(functools.partial(spread_kernel, flip, len(after), line),...  32.3 us
    pallas_call x6, Pallas kernels, place(): pl.pallas_call(functools.partial(place_kernel, len(after), n, into is not...  32.1 us
    ppermute x18, starting transfers between devices, gather_parts(): got = lax.ppermute(value, 'tensor', swap_pairs(first, last))  30.4 us
    pallas_call x1, Pallas kernels, forward(): pl.pallas_call(functools.partial(forward_kernel, ranges), grid_spec=pltpu...  14.2 us
  transfers between devices with their start and end apart: 61, of which 20 were waited for; matrix products, arithmetic and copies ran while one was open for 3% of the time, Pallas kernels for 30%

profile of v4, /device:TPU:0, one launch (start us, length us, event | category | flops | bytes accessed | tf_op | source)
XLA Modules:
  0.0 354.4 jit_solution(2431729628680647933)
XLA Ops:
  0.6 5.0 %collective-permute-start = (bf16[256,1024]{1,0:T(8,128)(2,1)}, bf16[256,1024]{1,0:T(8,128)(2,1)S(1)}, u32[]{:S(2)}, u32[]{:S(2)}) collective-permute-start(bf16[256,1024]{1,0:T(8,128)(2,1)} %refs_1_.7), channel_id=1, source_target_pairs={{0,2},{1,3},{2,4},{3,5},{4,6},{5,7},{8,10},{9,11},{10,12},{11,13},... | collective-permute-start | bytes 1572872 | tf_op jit(solution)/shard_map/ppermute | solution.py:60
  35.9 7.6 %collective-permute-done.4.refs_5_.refs_6_ = bf16[256,1024]{1,0:T(8,128)(2,1)S(1)} collective-permute-done((bf16[256,1024]{1,0:T(8,128)(2,1)S(1)}, bf16[256,1024]{1,0:T(8,128)(2,1)S(1)}, u32[]{:S(2)}, u32[]{:S(2)}) %collective-permute-start.4) | collective-permute-done | bytes 524320 | tf_op jit(solution)/shard_map/ppermute | solution.py:61
  52.7 8.5 %collective-permute-done.19.refs_22_ = bf16[256,1024]{1,0:T(8,128)(2,1)S(1)} collective-permute-done((bf16[256,1024]{1,0:T(8,128)(2,1)S(1)}, bf16[256,1024]{1,0:T(8,128)(2,1)S(1)}, u32[]{:S(2)}, u32[]{:S(2)}) %collective-permute-start.19) | collective-permute-done | bytes 524320 | tf_op jit(solution)/shard_map/ppermute | solution.py:61
  67.9 7.0 %collective-permute-done.8.refs_9_.refs_10_ = bf16[256,1024]{1,0:T(8,128)(2,1)} collective-permute-done((bf16[256,1024]{1,0:T(8,128)(2,1)S(1)}, bf16[256,1024]{1,0:T(8,128)(2,1)}, u32[]{:S(2)}, u32[]{:S(2)}) %collective-permute-start.8) | collective-permute-done | bytes 524320 | tf_op jit(solution)/shard_map/ppermute | solution.py:61
  84.4 8.2 %collective-permute-done.23.refs_26_ = bf16[256,1024]{1,0:T(8,128)(2,1)} collective-permute-done((bf16[256,1024]{1,0:T(8,128)(2,1)S(1)}, bf16[256,1024]{1,0:T(8,128)(2,1)}, u32[]{:S(2)}, u32[]{:S(2)}) %collective-permute-start.23) | collective-permute-done | bytes 524320 | tf_op jit(solution)/shard_map/ppermute | solution.py:61
  104.4 14.2 %forward_rows.1 = (bf16[32,256,128]{2,1,0:T(8,128)(2,1)}, f32[32,256,128]{2,1,0:T(8,128)}) custom-call(s32[3]{0:T(128)} %pad_add_fusion.meta, s32[256]{0:T(256)} %reshape.55.pat, bf16[256,1024]{1,0:T(8,128)(2,1)} %refs_1_.7, bf16[256,1024]{1,0:T(8,128)(2,1)} %copy-done, bf16[256,1024]{1,0:T(8,128)(2,1)} %copy-done.1, bf16[256,1024]{1,0:T(8,128)(2,1)} %copy-done.2, ...), custom_call_target="tpu_custom_call" | custom-call | flops 3000000000 | bytes 1000 | tf_op jit(solution)/shard_map/forward_rows/pallas_call | solution.py:227
  118.6 8.7 %grad_rows.4 = (bf16[4,8,128,128]{3,2,1,0:T(8,128)(2,1)}, bf16[4,8,128,128]{3,2,1,0:T(8,128)(2,1)}, bf16[32,256,128]{2,1,0:T(8,128)(2,1)}) custom-call(s32[3]{0:T(128)} %pad_add_fusion.meta, s32[256]{0:T(256)} %reshape.55.pat, bf16[32,256,128]{2,1,0:T(8,128)(2,1)} %get-tuple-element.139.refs_0_.refs_33_.refs_1_, bf16[256,1024]{1,0:T(8,128)(2,1)} %refs_1_.7, ...), custom_call_target="tpu_custom_call" | custom-call | flops 1000 | bytes 1000 | tf_op jit(solution)/shard_map/grad_rows/pallas_call | solution.py:408
  132.7 9.5 %grad_rows.5 = (bf16[2,4,8,128,128]{4,3,2,1,0:T(8,128)(2,1)}, bf16[32,256,128]{2,1,0:T(8,128)(2,1)}) custom-call(s32[3]{0:T(128)} %pad_add_fusion.meta, s32[256]{0:T(256)} %reshape.55.pat, bf16[4,8,128,128]{3,2,1,0:T(8,128)(2,1)} %get-tuple-element.154.refs_0_, bf16[256,1024]{1,0:T(8,128)(2,1)} %refs_1_.7, ...), custom_call_target="tpu_custom_call", output_to_operand_aliasing={{1}: (40, {})} | custom-call | flops 1000 | bytes 1000 | tf_op jit(solution)/shard_map/grad_rows/pallas_call | solution.py:408
  143.7 14.7 %grad_rows.6 = (bf16[6,8,128,128]{3,2,1,0:T(8,128)(2,1)}, bf16[6,8,128,128]{3,2,1,0:T(8,128)(2,1)}, bf16[6,8,128,128]{3,2,1,0:T(8,128)(2,1)}, bf16[6,8,128,128]{3,2,1,0:T(8,128)(2,1)}, bf16[32,256,128]{2,1,0:T(8,128)(2,1)}) custom-call(s32[3]{0:T(128)} %pad_add_fusion.meta, s32[256]{0:T(256)} %reshape.55.pat, ...), custom_call_target="tpu_custom_call", output_to_operand_aliasing={{4}: (38, {})} | custom-call | flops 1000 | bytes 1000 | tf_op jit(solution)/shard_map/grad_rows/pallas_call | solution.py:408
  159.5 15.8 %spread_out.1 = (bf16[4,256,1024]{2,1,0:T(8,128)(2,1)}, bf16[2,256,1024]{2,1,0:T(8,128)(2,1)}, bf16[2,256,1024]{2,1,0:T(8,128)(2,1)}) custom-call(s32[3]{0:T(128)} %pad_add_fusion.meta, s32[256]{0:T(256)} %reshape.55.pat, bf16[6,8,128,128]{3,2,1,0:T(8,128)(2,1)} %get-tuple-element.159.refs_0_, ...), custom_call_target="tpu_custom_call" | custom-call | flops 1000 | bytes 1000 | tf_op jit(solution)/shard_map/spread_out/pallas_call | solution.py:287
  177.1 16.5 %grad_rows.7 = (bf16[2,6,8,128,128]{4,3,2,1,0:T(8,128)(2,1)}, bf16[2,6,8,128,128]{4,3,2,1,0:T(8,128)(2,1)}, bf16[32,256,128]{2,1,0:T(8,128)(2,1)}) custom-call(s32[3]{0:T(128)} %pad_add_fusion.meta, s32[256]{0:T(256)} %reshape.55.pat, bf16[4,256,1024]{2,1,0:T(8,128)(2,1)} %get-tuple-element.202.refs_0_, ...), custom_call_target="tpu_custom_call", output_to_operand_aliasing={{2}: (42, {})} | custom-call | flops 1000 | bytes 1000 | tf_op jit(solution)/shard_map/grad_rows/pallas_call | solution.py:408
  200.2 16.5 %spread_back.1 = (bf16[4,256,1024]{2,1,0:T(8,128)(2,1)}, bf16[2,256,1024]{2,1,0:T(8,128)(2,1)}, bf16[2,256,1024]{2,1,0:T(8,128)(2,1)}) custom-call(s32[3]{0:T(128)} %pad_add_fusion.meta, s32[256]{0:T(256)} %reshape.55.pat, s32[8,128]{1,0:T(8,128)} %get-tuple-element.169.refs_0_, bf16[32,256,128]{2,1,0:T(8,128)(2,1)} %get-tuple-element.170.refs_1_, ...), custom_call_target="tpu_custom_call" | custom-call | flops 1000 | bytes 1000 | tf_op jit(solution)/shard_map/spread_back/pallas_call | solution.py:287
  223.2 9.7 %collective-permute-done.39 = bf16[256,1024]{1,0:T(8,128)(2,1)S(1)} collective-permute-done((bf16[256,1024]{1,0:T(8,128)(2,1)S(1)}, bf16[256,1024]{1,0:T(8,128)(2,1)S(1)}, u32[]{:S(2)}, u32[]{:S(2)}) %collective-permute-start.39) | collective-permute-done | bytes 524320 | tf_op jit(solution)/shard_map/ppermute | solution.py:135
  240.7 7.3 %collective-permute-done.41 = bf16[256,1024]{1,0:T(8,128)(2,1)S(1)} collective-permute-done((bf16[256,1024]{1,0:T(8,128)(2,1)S(1)}, bf16[256,1024]{1,0:T(8,128)(2,1)S(1)}, u32[]{:S(2)}, u32[]{:S(2)}) %collective-permute-start.41) | collective-permute-done | bytes 524320 | tf_op jit(solution)/shard_map/ppermute | solution.py:135
  249.6 11.1 %collective-permute-start.43 = (bf16[256,1024]{1,0:T(8,128)(2,1)S(1)}, bf16[256,1024]{1,0:T(8,128)(2,1)S(1)}, u32[]{:S(2)}, u32[]{:S(2)}) collective-permute-start(bf16[256,1024]{1,0:T(8,128)(2,1)S(1)} %get-tuple-element.194.refs_1_), channel_id=1, source_target_pairs={{0,2},{1,3},{2,4},{3,5},{4,6},{5,7},{8,10},{9,11},{10,12},{11,13},... | collective-permute-start | bytes 1572872 | tf_op jit(solution)/shard_map/ppermute | solution.py:135
  269.9 6.3 %collective-permute-start.48 = (bf16[256,1024]{1,0:T(8,128)(2,1)S(1)}, bf16[256,1024]{1,0:T(8,128)(2,1)}, u32[]{:S(2)}, u32[]{:S(2)}) collective-permute-start(bf16[256,1024]{1,0:T(8,128)(2,1)S(1)} %get-tuple-element.253.refs_0_), channel_id=1, source_target_pairs={{0,2},{1,3},{8,10},{9,11},{16,18},{17,19},{24,26},{25,27}} | collective-permute-start | bytes 1572872 | tf_op jit(solution)/shard_map/ppermute | solution.py:135
  277.7 7.2 %place_rows.7 = (s32[8,128]{1,0:T(8,128)}, bf16[32,8,128,128]{3,2,1,0:T(8,128)(2,1)}, bf16[32,8,128,128]{3,2,1,0:T(8,128)(2,1)}, bf16[6,8,128,128]{3,2,1,0:T(8,128)(2,1)}, bf16[6,8,128,128]{3,2,1,0:T(8,128)(2,1)}) custom-call(s32[3]{0:T(128)} %pad_add_fusion.meta, bf16[256,1024]{1,0:T(8,128)(2,1)} %copy-done.27, ...), custom_call_target="tpu_custom_call", output_to_operand_aliasing={{1}: (8, {}), {2}: (9, {})} | custom-call | flops 1000 | bytes 1000 | tf_op jit(solution)/shard_map/place_rows/pallas_call | solution.py:468
  289.6 6.9 %collective-permute-start.50 = (bf16[256,1024]{1,0:T(8,128)(2,1)S(1)}, bf16[256,1024]{1,0:T(8,128)(2,1)S(1)}, u32[]{:S(2)}, u32[]{:S(2)}) collective-permute-start(bf16[256,1024]{1,0:T(8,128)(2,1)S(1)} %get-tuple-element.251.refs_0_), channel_id=1, source_target_pairs={{0,2},{1,3},{2,4},{3,5},{8,10},{9,11},{10,12},{11,13},{16,18},{17,... | collective-permute-start | bytes 1572872 | tf_op jit(solution)/shard_map/ppermute | solution.py:135
  300.5 7.8 %collective-permute-done.50 = bf16[256,1024]{1,0:T(8,128)(2,1)S(1)} collective-permute-done((bf16[256,1024]{1,0:T(8,128)(2,1)S(1)}, bf16[256,1024]{1,0:T(8,128)(2,1)S(1)}, u32[]{:S(2)}, u32[]{:S(2)}) %collective-permute-start.50) | collective-permute-done | bytes 524320 | tf_op jit(solution)/shard_map/ppermute | solution.py:135
  308.9 8.4 %collective-permute-start.54 = (bf16[256,1024]{1,0:T(8,128)(2,1)S(1)}, bf16[256,1024]{1,0:T(8,128)(2,1)S(1)}, u32[]{:S(2)}, u32[]{:S(2)}) collective-permute-start(bf16[256,1024]{1,0:T(8,128)(2,1)S(1)} %get-tuple-element.231.refs_1_), channel_id=1, source_target_pairs={{0,2},{1,3},{2,4},{3,5},{4,6},{5,7},{8,10},{9,11},{10,12},{11,13},... | collective-permute-start | bytes 1572872 | tf_op jit(solution)/shard_map/ppermute | solution.py:135
  319.2 8.9 %collective-permute-done.54 = bf16[256,1024]{1,0:T(8,128)(2,1)S(1)} collective-permute-done((bf16[256,1024]{1,0:T(8,128)(2,1)S(1)}, bf16[256,1024]{1,0:T(8,128)(2,1)S(1)}, u32[]{:S(2)}, u32[]{:S(2)}) %collective-permute-start.54) | collective-permute-done | bytes 524320 | tf_op jit(solution)/shard_map/ppermute | solution.py:135
  333.3 7.1 %place_rows.9 = (s32[8,128]{1,0:T(8,128)}, bf16[32,8,128,128]{3,2,1,0:T(8,128)(2,1)}, bf16[32,8,128,128]{3,2,1,0:T(8,128)(2,1)}, bf16[6,8,128,128]{3,2,1,0:T(8,128)(2,1)}, bf16[6,8,128,128]{3,2,1,0:T(8,128)(2,1)}) custom-call(s32[3]{0:T(128)} %pad_add_fusion.meta, bf16[256,1024]{1,0:T(8,128)(2,1)} %fusion.13.refs_0_, ...), custom_call_target="tpu_custom_call", output_to_operand_aliasing={{1}: (6, {}), {2}: (7, {})} | custom-call | flops 1000 | bytes 1000 | tf_op jit(solution)/shard_map/place_rows/pallas_call | solution.py:468
  342.7 5.0 %place_rows.10 = (s32[8,128]{1,0:T(8,128)}, bf16[32,8,128,128]{3,2,1,0:T(8,128)(2,1)}, bf16[32,8,128,128]{3,2,1,0:T(8,128)(2,1)}) custom-call(s32[3]{0:T(128)} %pad_add_fusion.meta, s32[8,128]{1,0:T(8,128)} %get-tuple-element.236.refs_0_, bf16[6,8,128,128]{3,2,1,0:T(8,128)(2,1)} %copy-done.33, ...), custom_call_target="tpu_custom_call", output_to_operand_aliasing={{1}: (4, {}), {2}: (5, {})} | custom-call | flops 1000 | bytes 1000 | tf_op jit(solution)/shard_map/place_rows/pallas_call | solution.py:468
  349.4 5.0 %place_rows.11 = (s32[8,128]{1,0:T(8,128)}, bf16[32,8,128,128]{3,2,1,0:T(8,128)(2,1)}, bf16[32,8,128,128]{3,2,1,0:T(8,128)(2,1)}) custom-call(s32[3]{0:T(128)} %pad_add_fusion.meta, s32[8,128]{1,0:T(8,128)} %get-tuple-element.241.refs_0_, bf16[6,8,128,128]{3,2,1,0:T(8,128)(2,1)} %copy-done.35, ...), custom_call_target="tpu_custom_call", output_to_operand_aliasing={{1}: (4, {}), {2}: (5, {})} | custom-call | flops 1000 | bytes 1000 | tf_op jit(solution)/shard_map/place_rows/pallas_call | solution.py:468
  (206 shorter events, 129.9 us)
Async XLA Ops:
  0.6 17.6 %collective-permute-start = (bf16[256,1024]{1,0:T(8,128)(2,1)}, bf16[256,1024]{1,0:T(8,128)(2,1)S(1)}, u32[]{:S(2)}, u32[]{:S(2)}) collective-permute-start(bf16[256,1024]{1,0:T(8,128)(2,1)} %refs_1_.7), channel_id=1, source_target_pairs={{0,2},{1,3},{2,4},{3,5},{4,6},{5,7},{8,10},{9,11},{10,12},{11,13},... | collective-permute-start | bytes 1572872 | tf_op jit(solution)/shard_map/ppermute | solution.py:60
  8.5 19.8 %collective-permute-start.15 = (bf16[256,1024]{1,0:T(8,128)(2,1)}, bf16[256,1024]{1,0:T(8,128)(2,1)S(1)}, u32[]{:S(2)}, u32[]{:S(2)}) collective-permute-start(bf16[256,1024]{1,0:T(8,128)(2,1)} %refs_17_.7), channel_id=1, source_target_pairs={{0,2},{1,3},{2,4},{3,5},{4,6},{5,7},{8,10},{9,11},{10,12},{11,13},... | collective-permute-start | bytes 1572872 | tf_op jit(solution)/shard_map/ppermute | solution.py:60
  13.0 20.8 %collective-permute-start.16 = (bf16[256,1024]{1,0:T(8,128)(2,1)}, bf16[256,1024]{1,0:T(8,128)(2,1)S(1)}, u32[]{:S(2)}, u32[]{:S(2)}) collective-permute-start(bf16[256,1024]{1,0:T(8,128)(2,1)} %refs_17_.7), channel_id=1, source_target_pairs={{2,0},{3,1},{4,2},{5,3},{6,4},{7,5},{10,8},{11,9},{12,10},{13,11},... | collective-permute-start | bytes 1572872 | tf_op jit(solution)/shard_map/ppermute | solution.py:61
  23.3 20.3 %collective-permute-start.4 = (bf16[256,1024]{1,0:T(8,128)(2,1)S(1)}, bf16[256,1024]{1,0:T(8,128)(2,1)S(1)}, u32[]{:S(2)}, u32[]{:S(2)}) collective-permute-start(bf16[256,1024]{1,0:T(8,128)(2,1)S(1)} %collective-permute-done.1.refs_2_.refs_3_), channel_id=1, source_target_pairs={{2,0},{3,1},{4,2},{5,3},{10,8},{11,9},{12,10},{13,11},{18,16},{19,... | collective-permute-start | bytes 1572872 | tf_op jit(solution)/shard_map/ppermute | solution.py:61
  74.9 17.7 %collective-permute-start.23 = (bf16[256,1024]{1,0:T(8,128)(2,1)S(1)}, bf16[256,1024]{1,0:T(8,128)(2,1)}, u32[]{:S(2)}, u32[]{:S(2)}) collective-permute-start(bf16[256,1024]{1,0:T(8,128)(2,1)S(1)} %collective-permute-done.19.refs_22_), channel_id=1, source_target_pairs={{2,0},{3,1},{10,8},{11,9},{18,16},{19,17},{26,24},{27,25}} | collective-permute-start | bytes 1572872 | tf_op jit(solution)/shard_map/ppermute | solution.py:61
  79.5 24.9 %collective-permute-start.13 = (bf16[256,1024]{1,0:T(8,128)(2,1)}, bf16[256,1024]{1,0:T(8,128)(2,1)}, u32[]{:S(2)}, u32[]{:S(2)}) collective-permute-start(bf16[256,1024]{1,0:T(8,128)(2,1)} %collective-permute-done.8.refs_9_.refs_10_), channel_id=1, source_target_pairs={{0,1},{1,0},{8,9},{9,8},{16,17},{17,16},{24,25},{25,24}} | collective-permute-start | bytes 1572872 | tf_op jit(solution)/shard_map/ppermute | solution.py:75
  82.9 21.4 %collective-permute-start.14 = (bf16[256,1024]{1,0:T(8,128)(2,1)}, bf16[256,1024]{1,0:T(8,128)(2,1)}, u32[]{:S(2)}, u32[]{:S(2)}) collective-permute-start(bf16[256,1024]{1,0:T(8,128)(2,1)} %collective-permute-done.7.refs_8_.refs_9_), channel_id=1, source_target_pairs={{6,7},{7,6},{14,15},{15,14},{22,23},{23,22},{30,31},{31,30}} | collective-permute-start | bytes 1572872 | tf_op jit(solution)/shard_map/ppermute | solution.py:75
  93.0 25.5 %collective-permute-start.28 = (bf16[256,1024]{1,0:T(8,128)(2,1)}, bf16[256,1024]{1,0:T(8,128)(2,1)}, u32[]{:S(2)}, u32[]{:S(2)}) collective-permute-start(bf16[256,1024]{1,0:T(8,128)(2,1)} %collective-permute-done.23.refs_26_), channel_id=1, source_target_pairs={{0,1},{1,0},{8,9},{9,8},{16,17},{17,16},{24,25},{25,24}} | collective-permute-start | bytes 1572872 | tf_op jit(solution)/shard_map/ppermute | solution.py:75
  96.1 22.5 %collective-permute-start.29 = (bf16[256,1024]{1,0:T(8,128)(2,1)}, bf16[256,1024]{1,0:T(8,128)(2,1)}, u32[]{:S(2)}, u32[]{:S(2)}) collective-permute-start(bf16[256,1024]{1,0:T(8,128)(2,1)} %collective-permute-done.22.refs_25_), channel_id=1, source_target_pairs={{6,7},{7,6},{14,15},{15,14},{22,23},{23,22},{30,31},{31,30}} | collective-permute-start | bytes 1572872 | tf_op jit(solution)/shard_map/ppermute | solution.py:75
  142.2 51.5 %collective-permute-start.38 = (bf16[2,4,8,128,128]{4,3,2,1,0:T(8,128)(2,1)}, bf16[2,4,8,128,128]{4,3,2,1,0:T(8,128)(2,1)S(1)}, u32[]{:S(2)}, u32[]{:S(2)}) collective-permute-start(bf16[2,4,8,128,128]{4,3,2,1,0:T(8,128)(2,1)} %get-tuple-element.157.refs_0_.refs_1_), channel_id=1, source_target_pairs={{0,16},{8,24},{16,0},{24,8},{1,17},{9,25},{17,1},{25,9},{2,18},{10... | collective-permute-start | bytes 6291464 | tf_op jit(solution)/shard_map/ppermute | solution.py:162
  158.5 17.4 %collective-permute-start.35 = (bf16[6,8,128,128]{3,2,1,0:T(8,128)(2,1)}, bf16[6,8,128,128]{3,2,1,0:T(8,128)(2,1)S(1)}, u32[]{:S(2)}, u32[]{:S(2)}) collective-permute-start(bf16[6,8,128,128]{3,2,1,0:T(8,128)(2,1)} %get-tuple-element.163), channel_id=1, source_target_pairs={{0,8},{8,0},{16,24},{24,16},{1,9},{9,1},{17,25},{25,17},{2,10},{10... | collective-permute-start | bytes 4718600 | tf_op jit(solution)/shard_map/ppermute | solution.py:155
  175.3 41.4 %collective-permute-start.33 = (bf16[2,256,1024]{2,1,0:T(8,128)(2,1)}, bf16[2,256,1024]{2,1,0:T(8,128)(2,1)S(1)}, u32[]{:S(2)}, u32[]{:S(2)}) collective-permute-start(bf16[2,256,1024]{2,1,0:T(8,128)(2,1)} %get-tuple-element.162), channel_id=1, source_target_pairs={{0,1},{1,0},{2,3},{3,2},{4,5},{5,4},{6,7},{7,6},{8,9},{9,8},{10,11... | collective-permute-start | bytes 3145736 | tf_op jit(solution)/shard_map/ppermute | solution.py:111
  193.7 82.5 %collective-permute-start.46 = (bf16[2,6,8,128,128]{4,3,2,1,0:T(8,128)(2,1)}, bf16[2,6,8,128,128]{4,3,2,1,0:T(8,128)(2,1)}, u32[]{:S(2)}, u32[]{:S(2)}) collective-permute-start(bf16[2,6,8,128,128]{4,3,2,1,0:T(8,128)(2,1)} %get-tuple-element.198.refs_0_.refs_5_), channel_id=1, source_target_pairs={{0,16},{8,24},{16,0},{24,8},{1,17},{9,25},{17,1},{25,9},{2,18},{10... | collective-permute-start | bytes 9437192 | tf_op jit(solution)/shard_map/ppermute | solution.py:162
  194.3 28.9 %collective-permute-start.32 = (bf16[2,256,1024]{2,1,0:T(8,128)(2,1)S(1)}, bf16[2,256,1024]{2,1,0:T(8,128)(2,1)S(1)}, u32[]{:S(2)}, u32[]{:S(2)}) collective-permute-start(bf16[2,256,1024]{2,1,0:T(8,128)(2,1)S(1)} %copy-done.40), channel_id=1, source_target_pairs={{0,1},{1,0},{2,3},{3,2},{4,5},{5,4},{6,7},{7,6},{8,9},{9,8},{10,11... | collective-permute-start | bytes 3145736 | tf_op jit(solution)/shard_map/ppermute | solution.py:111
  238.4 26.2 %collective-permute-start.45 = (bf16[2,256,1024]{2,1,0:T(8,128)(2,1)S(1)}, bf16[2,256,1024]{2,1,0:T(8,128)(2,1)S(1)}, u32[]{:S(2)}, u32[]{:S(2)}) collective-permute-start(bf16[2,256,1024]{2,1,0:T(8,128)(2,1)S(1)} %copy-done.41), channel_id=1, source_target_pairs={{0,1},{1,0},{2,3},{3,2},{4,5},{5,4},{6,7},{7,6},{8,9},{9,8},{10,11... | collective-permute-start | bytes 3145736 | tf_op jit(solution)/shard_map/ppermute | solution.py:111
  239.2 94.1 %collective-permute-start.56 = (bf16[2,6,8,128,128]{4,3,2,1,0:T(8,128)(2,1)}, bf16[2,6,8,128,128]{4,3,2,1,0:T(8,128)(2,1)}, u32[]{:S(2)}, u32[]{:S(2)}) collective-permute-start(bf16[2,6,8,128,128]{4,3,2,1,0:T(8,128)(2,1)} %get-tuple-element.233.refs_3_), channel_id=1, source_target_pairs={{0,16},{8,24},{16,0},{24,8},{1,17},{9,25},{17,1},{25,9},{2,18},{10... | collective-permute-start | bytes 9437192 | tf_op jit(solution)/shard_map/ppermute | solution.py:162
  248.0 37.0 %collective-permute-start.47 = (bf16[2,256,1024]{2,1,0:T(8,128)(2,1)}, bf16[2,256,1024]{2,1,0:T(8,128)(2,1)S(1)}, u32[]{:S(2)}, u32[]{:S(2)}) collective-permute-start(bf16[2,256,1024]{2,1,0:T(8,128)(2,1)} %get-tuple-element.206), channel_id=1, source_target_pairs={{0,1},{1,0},{2,3},{3,2},{4,5},{5,4},{6,7},{7,6},{8,9},{9,8},{10,11... | collective-permute-start | bytes 3145736 | tf_op jit(solution)/shard_map/ppermute | solution.py:111
  249.6 20.3 %collective-permute-start.43 = (bf16[256,1024]{1,0:T(8,128)(2,1)S(1)}, bf16[256,1024]{1,0:T(8,128)(2,1)S(1)}, u32[]{:S(2)}, u32[]{:S(2)}) collective-permute-start(bf16[256,1024]{1,0:T(8,128)(2,1)S(1)} %get-tuple-element.194.refs_1_), channel_id=1, source_target_pairs={{0,2},{1,3},{2,4},{3,5},{4,6},{5,7},{8,10},{9,11},{10,12},{11,13},... | collective-permute-start | bytes 1572872 | tf_op jit(solution)/shard_map/ppermute | solution.py:135
  264.6 20.3 %collective-permute-start.44 = (bf16[256,1024]{1,0:T(8,128)(2,1)}, bf16[256,1024]{1,0:T(8,128)(2,1)}, u32[]{:S(2)}, u32[]{:S(2)}) collective-permute-start(bf16[256,1024]{1,0:T(8,128)(2,1)} %get-tuple-element.254), channel_id=1, source_target_pairs={{2,0},{3,1},{4,2},{5,3},{6,4},{7,5},{10,8},{11,9},{12,10},{13,11},... | collective-permute-start | bytes 1572872 | tf_op jit(solution)/shard_map/ppermute | solution.py:136
  269.9 18.0 %collective-permute-start.48 = (bf16[256,1024]{1,0:T(8,128)(2,1)S(1)}, bf16[256,1024]{1,0:T(8,128)(2,1)}, u32[]{:S(2)}, u32[]{:S(2)}) collective-permute-start(bf16[256,1024]{1,0:T(8,128)(2,1)S(1)} %get-tuple-element.253.refs_0_), channel_id=1, source_target_pairs={{0,2},{1,3},{8,10},{9,11},{16,18},{17,19},{24,26},{25,27}} | collective-permute-start | bytes 1572872 | tf_op jit(solution)/shard_map/ppermute | solution.py:135
  289.6 18.7 %collective-permute-start.50 = (bf16[256,1024]{1,0:T(8,128)(2,1)S(1)}, bf16[256,1024]{1,0:T(8,128)(2,1)S(1)}, u32[]{:S(2)}, u32[]{:S(2)}) collective-permute-start(bf16[256,1024]{1,0:T(8,128)(2,1)S(1)} %get-tuple-element.251.refs_0_), channel_id=1, source_target_pairs={{0,2},{1,3},{2,4},{3,5},{8,10},{9,11},{10,12},{11,13},{16,18},{17,... | collective-permute-start | bytes 1572872 | tf_op jit(solution)/shard_map/ppermute | solution.py:135
  308.9 19.2 %collective-permute-start.54 = (bf16[256,1024]{1,0:T(8,128)(2,1)S(1)}, bf16[256,1024]{1,0:T(8,128)(2,1)S(1)}, u32[]{:S(2)}, u32[]{:S(2)}) collective-permute-start(bf16[256,1024]{1,0:T(8,128)(2,1)S(1)} %get-tuple-element.231.refs_1_), channel_id=1, source_target_pairs={{0,2},{1,3},{2,4},{3,5},{4,6},{5,7},{8,10},{9,11},{10,12},{11,13},... | collective-permute-start | bytes 1572872 | tf_op jit(solution)/shard_map/ppermute | solution.py:135
  318.6 22.4 %collective-permute-start.57 = (bf16[6,8,128,128]{3,2,1,0:T(8,128)(2,1)}, bf16[6,8,128,128]{3,2,1,0:T(8,128)(2,1)S(1)}, u32[]{:S(2)}, u32[]{:S(2)}) collective-permute-start(bf16[6,8,128,128]{3,2,1,0:T(8,128)(2,1)} %get-tuple-element.237), channel_id=1, source_target_pairs={{0,8},{8,0},{16,24},{24,16},{1,9},{9,1},{17,25},{25,17},{2,10},{10... | collective-permute-start | bytes 4718600 | tf_op jit(solution)/shard_map/ppermute | solution.py:155
  318.7 22.3 %collective-permute-start.58 = (bf16[6,8,128,128]{3,2,1,0:T(8,128)(2,1)}, bf16[6,8,128,128]{3,2,1,0:T(8,128)(2,1)S(1)}, u32[]{:S(2)}, u32[]{:S(2)}) collective-permute-start(bf16[6,8,128,128]{3,2,1,0:T(8,128)(2,1)} %get-tuple-element.238), channel_id=1, source_target_pairs={{0,8},{8,0},{16,24},{24,16},{1,9},{9,1},{17,25},{25,17},{2,10},{10... | collective-permute-start | bytes 4718600 | tf_op jit(solution)/shard_map/ppermute | solution.py:155
  (79 other events, 1532.5 us)
